TPU v7x, 32 devices: a whole 2x2x4 slice. The times are simulated.
32 devices in a mesh: groups: 2 (over x), expert: 16 (over z, y, core).
Axes of the slice: x: 2, y: 2, z: 4, core: 2. Of those that a mesh axis runs over, the one named last changes fastest.
Arguments:
- tokens: bfloat16 [4096, 7168], P(('groups', 'expert')), parts along dimension 0, may hold values from -6 to 6
- out_grad: bfloat16 [4096, 7168], P(('groups', 'expert')), parts along dimension 0, may hold values from -6 to 6
- routes: int32 [4096, 8], P(('groups', 'expert')), parts along dimension 0, may hold values from 0 to 255, as said below
- gate_probs: float32 [4096, 8], P(('groups', 'expert')), parts along dimension 0, may hold values from 0.1 to 1
- w_gate: bfloat16 [7168, 2048], P(None, 'expert'), may hold values from -0.0625 to 0.0625
- w_up: bfloat16 [7168, 2048], P(None, 'expert'), may hold values from -0.0625 to 0.0625
- w_down: bfloat16 [2048, 7168], P('expert'), may hold values from -0.125 to 0.125
Outputs:
- layer_out: bfloat16 [4096, 7168], P(('groups', 'expert')), parts along dimension 0
- input_grad: bfloat16 [4096, 7168], P(('groups', 'expert')), parts along dimension 0
- prob_grad: float32 [4096, 8], P(('groups', 'expert')), parts along dimension 0
There are 2 independent parts, one for each index of `groups`. A program takes and returns all parts, laid end to end along the dimension named above; an argument that names none is the same for every part. Nothing has to cross between parts.
Inputs may be any that keep to these rules, and one draw needn't show every extreme that they name: `routes`: each row names 8 different experts. Among the 128 rows of one device, each expert id below 1 is named by 1 to 4 rows. In every draw each id below 1 is named by exactly 4 rows on some device, and some id below 1 is named by exactly 4 rows on every device.
All inputs are finite; a program needn't handle non-finite values.
Results may differ from a plain program's by a relative error of at most 0.0057.
Values may be sent and summed in bfloat16 or wider, within the bound.
No kernel may reach another device: no remote copies, remote signals or barrier semaphores. Data moves between devices by JAX's collectives and lax.ppermute only.
A program may use at most 64 MiB of HBM per device.

v0:
```python
import jax
import jax.numpy as jnp
from jax import lax
from jax.sharding import PartitionSpec as P

HID = 2048
PANEL = 128
CAP = 4


def slot_tables(routes, gate_probs, experts):
    expert_ids = jnp.arange(experts, dtype=jnp.int32)
    matches = routes[:, :, None] == expert_ids[None, None, :]
    per_token = jnp.sum(matches.astype(jnp.int32), axis=1)
    slot_order = jnp.cumsum(per_token, axis=0) - per_token
    slot_ids = jnp.arange(CAP, dtype=jnp.int32)
    placement = (per_token[:, :, None] == 1) & (slot_order[:, :, None] == slot_ids[None, None, :])
    placement = placement.astype(jnp.float32)
    route_prob = jnp.sum(jnp.where(matches, gate_probs[:, :, None], 0.0), axis=1)
    slot_prob = jnp.sum(placement * route_prob[:, :, None], axis=0).reshape(-1)
    return (matches, placement, slot_prob)


def expert_compute(token_rows, grad_rows, w_gate, w_up, w_down):
    gate_pre = jnp.dot(token_rows, w_gate, preferred_element_type=jnp.float32)
    up_pre = jnp.dot(token_rows, w_up, preferred_element_type=jnp.float32)
    sigmoid_gate = jax.nn.sigmoid(gate_pre)
    silu_gate = gate_pre * sigmoid_gate
    hidden = (silu_gate * up_pre).astype(jnp.bfloat16)
    expert_out = jnp.dot(hidden, w_down, preferred_element_type=jnp.float32).astype(jnp.bfloat16)
    contract = (((1,), (1,)), ((), ()))
    hidden_grad = lax.dot_general(grad_rows, w_down, contract, preferred_element_type=jnp.float32)
    silu_slope = sigmoid_gate * (1.0 + gate_pre * (1.0 - sigmoid_gate))
    gate_grad = (hidden_grad * up_pre * silu_slope).astype(jnp.bfloat16)
    up_grad = (hidden_grad * silu_gate).astype(jnp.bfloat16)
    input_part = lax.dot_general(gate_grad, w_gate, contract, preferred_element_type=jnp.float32)
    input_part = input_part + lax.dot_general(
        up_grad, w_up, contract, preferred_element_type=jnp.float32
    )
    return (expert_out, input_part.astype(jnp.bfloat16))


def run_slots(token_rows, grad_rows, w_gate, w_up, w_down):
    return expert_compute(token_rows, grad_rows, w_gate, w_up, w_down)


def expert_section(token_slots, grad_slots, w_gate, w_up, w_down):
    leading, items, model_width = token_slots.shape
    out_rows, input_rows = run_slots(
        token_slots.reshape(-1, model_width),
        grad_slots.reshape(-1, model_width),
        w_gate,
        w_up,
        w_down,
    )
    out_rows = out_rows.reshape(leading, items, model_width)
    input_rows = input_rows.reshape(leading, items, model_width)
    return (
        lax.all_to_all(out_rows, "expert", split_axis=0, concat_axis=0, tiled=True),
        lax.all_to_all(input_rows, "expert", split_axis=0, concat_axis=0, tiled=True),
    )


def local(tokens, out_grad, routes, gate_probs, w_gate, w_up, w_down):
    panels = HID // PANEL
    devices = lax.axis_size("expert")
    experts = devices // panels
    tok_count, model_width = tokens.shape
    slot_total = experts * CAP
    matches, placement, slot_prob = slot_tables(routes, gate_probs, experts)
    placement_flat = placement.reshape(tok_count, slot_total)
    picker = placement_flat.T.astype(jnp.bfloat16)
    token_slots = jnp.dot(picker, tokens, preferred_element_type=jnp.float32).astype(jnp.bfloat16)
    grad_slots = jnp.dot(picker, out_grad, preferred_element_type=jnp.float32).astype(jnp.bfloat16)
    weighted_slots = (slot_prob[:, None] * grad_slots.astype(jnp.float32)).astype(jnp.bfloat16)

    def spread(slots):
        shaped = slots.reshape(experts, 1, CAP, model_width)
        return jnp.broadcast_to(shaped, (experts, panels, CAP, model_width)).reshape(
            devices, CAP, model_width
        )

    out_parts, input_parts = expert_section(
        lax.all_to_all(spread(token_slots), "expert", split_axis=0, concat_axis=0, tiled=True),
        lax.all_to_all(spread(weighted_slots), "expert", split_axis=0, concat_axis=0, tiled=True),
        w_gate,
        w_up,
        w_down,
    )
    out_sum = jnp.sum(
        out_parts.reshape(experts, panels, CAP, model_width), axis=1, dtype=jnp.float32
    ).reshape(slot_total, model_width)
    input_sum = jnp.sum(
        input_parts.reshape(experts, panels, CAP, model_width), axis=1, dtype=jnp.float32
    ).reshape(slot_total, model_width)
    highest = lax.Precision.HIGHEST
    mixing = placement_flat * slot_prob[None, :]
    layer_moe = jnp.dot(mixing, out_sum, precision=highest, preferred_element_type=jnp.float32)
    layer_out = (tokens.astype(jnp.float32) + layer_moe).astype(jnp.bfloat16)
    input_moe = jnp.dot(
        placement_flat, input_sum, precision=highest, preferred_element_type=jnp.float32
    )
    input_grad = (out_grad.astype(jnp.float32) + input_moe).astype(jnp.bfloat16)
    slot_dot = jnp.sum(grad_slots.astype(jnp.float32) * out_sum, axis=1)
    token_dot = jnp.sum(placement * slot_dot.reshape(experts, CAP)[None, :, :], axis=2)
    prob_grad = jnp.sum(jnp.where(matches, token_dot[:, None, :], 0.0), axis=2)
    return (layer_out, input_grad, prob_grad)


def solution(mesh):
    return jax.shard_map(
        local,
        mesh=mesh,
        in_specs=(
            P(("groups", "expert"), None),
            P(("groups", "expert"), None),
            P(("groups", "expert"), None),
            P(("groups", "expert"), None),
            P(None, "expert"),
            P(None, "expert"),
            P("expert", None),
        ),
        out_specs=(
            P(("groups", "expert"), None),
            P(("groups", "expert"), None),
            P(("groups", "expert"), None),
        ),
        check_vma=False,
    )
```

profile of v0, /device:TPU:0, one launch (start us, length us, event | category | flops | bytes accessed | tf_op | source)
XLA Modules:
  0.0 133.3 jit_solution(9760433735092513238)
XLA Ops:
  0.6 0.0 copy-start
  0.6 0.9 select_reduce_fusion
  1.5 0.1 copy.12
  1.6 0.2 reduce-window.7
  1.8 0.1 reduce.10
  1.9 1.9 %convolution_convert_fusion.2 = bf16[4,7168]{1,0:T(4,128)(2,1)S(1)} fusion(bf16[128,7168]{1,0:T(8,128)(2,1)} %param.7, s32[128]{0:T(128)S(1)} %sub.12, pred[128]{0:T(512)(128)(4,1)S(1)} %broadcast_compare_fusion.1), kind=kOutput, calls=%fused_computation.9 | convolution fusion | flops 7370752 | bytes 1892992 | tf_op jit(solution)/shard_map/dot_general | solution.py:73
  3.8 0.2 reshape.317
  4.0 29.8 %all_to_all.20 = bf16[16,4,7168]{2,1,0:T(4,128)(2,1)} all-to-all(bf16[16,4,7168]{2,1,0:T(4,128)(2,1)S(1)} %reshape.317), channel_id=1, replica_groups=mesh['groups'=2,'expert'=16] {'expert'}, dimensions={0} | all-to-all | bytes 1835008 | tf_op jit(solution)/shard_map/all_to_all | solution.py:84
  33.9 1.7 %reshape.318 = bf16[64,7168]{1,0:T(8,128)(2,1)S(1)} reshape(bf16[16,4,7168]{2,1,0:T(4,128)(2,1)} %all_to_all.20) | data formatting | bytes 1835008 | tf_op jit(solution)/shard_map/reshape | solution.py:50
  35.6 2.1 %fusion.29 = f32[64,128]{1,0:T(8,128)S(1)} fusion(bf16[64,7168]{1,0:T(8,128)(2,1)S(1)} %reshape.318, bf16[7168,128]{1,0:T(8,128)(2,1)} %param.11), kind=kOutput, calls=%fused_computation.50 | convolution fusion | flops 117440512 | bytes 2785280 | tf_op jit(solution)/shard_map/dot_general | solution.py:25
  37.7 0.5 fusion.30
  38.1 1.3 %convolution_convert_fusion = bf16[64,7168]{1,0:T(8,128)(2,1)} fusion(bf16[128,7168]{1,0:T(8,128)(2,1)S(1)} %copy-done, f32[64,128]{1,0:T(8,128)S(1)} %fusion.30, f32[64,128]{1,0:T(8,128)S(1)} %fusion.29), kind=kOutput, calls=%fused_computation.5 | convolution fusion | flops 117948416 | bytes 2818048 | tf_op jit(solution)/shard_map/dot_general | solution.py:30
  39.5 1.8 %reshape.319 = bf16[16,4,7168]{2,1,0:T(4,128)(2,1)S(1)} reshape(bf16[64,7168]{1,0:T(8,128)(2,1)} %convolution_convert_fusion) | data formatting | bytes 1835008 | tf_op jit(solution)/shard_map/reshape | solution.py:56
  41.3 27.0 %all_to_all.21 = bf16[16,4,7168]{2,1,0:T(4,128)(2,1)S(1)} all-to-all(bf16[16,4,7168]{2,1,0:T(4,128)(2,1)S(1)} %reshape.319), channel_id=1, replica_groups=mesh['groups'=2,'expert'=16] {'expert'}, dimensions={0} | all-to-all | bytes 1835008 | tf_op jit(solution)/shard_map/all_to_all | solution.py:59
  68.2 0.4 convert_reduce_fusion.1
  68.6 0.5 multiply_reduce_fusion
  69.1 0.1 select_reduce_fusion.1
  69.2 0.1 multiply_convert_fusion
  69.3 0.2 reshape.320
  69.6 26.8 %all_to_all.22 = bf16[16,4,7168]{2,1,0:T(4,128)(2,1)S(1)} all-to-all(bf16[16,4,7168]{2,1,0:T(4,128)(2,1)S(1)} %reshape.320), channel_id=1, replica_groups=mesh['groups'=2,'expert'=16] {'expert'}, dimensions={0} | all-to-all | bytes 1835008 | tf_op jit(solution)/shard_map/all_to_all | solution.py:85
  96.4 1.1 reshape.321
  97.5 2.1 %fusion.31 = f32[64,128]{1,0:T(8,128)S(1)} fusion(bf16[64,7168]{1,0:T(8,128)(2,1)} %reshape.321, bf16[128,7168]{1,0:T(8,128)(2,1)S(1)} %copy-done), kind=kOutput, calls=%fused_computation.52 | convolution fusion | flops 117440512 | bytes 2785280 | tf_op jit(solution)/shard_map/dot_general | solution.py:32
  99.6 0.8 fusion.15
  100.4 0.7 copy-done.3
  101.1 0.8 fusion.2
  101.9 1.3 reshape.322
  103.1 4.5 %all-to-all-start.3 = ((bf16[16,4,7168]{2,1,0:T(4,128)(2,1)}), bf16[16,4,7168]{2,1,0:T(4,128)(2,1)S(1)}, u32[]{:S(2)}, u32[]{:S(2)}) async-start(bf16[16,4,7168]{2,1,0:T(4,128)(2,1)} %reshape.322), calls=%async_computation.3 | async-start | bytes 1835008 | tf_op jit(solution)/shard_map/all_to_all | solution.py:60
  107.6 0.6 broadcast_select_fusion
  108.2 5.5 %fusion = bf16[128,7168]{1,0:T(8,128)(2,1)} fusion(f32[4,7168]{1,0:T(4,128)S(1)} %convert_reduce_fusion.1, bf16[128,7168]{1,0:T(8,128)(2,1)} %param.7, f32[4]{0:T(128)S(1)} %get-tuple-element.4, s32[128]{0:T(128)S(1)} %sub.12, pred[128]{0:T(512)(128)(4,1)S(1)} %broadcast_compare_fusion.1), kind=kOutput, calls=%fused_computation.2 | convolution fusion | flops 46794240 | bytes 3785360 | tf_op jit(solution)/shard_map/dot_general | solution.py:98
  113.7 14.8 %all-to-all-done.3 = bf16[16,4,7168]{2,1,0:T(4,128)(2,1)S(1)} async-done(((bf16[16,4,7168]{2,1,0:T(4,128)(2,1)}), bf16[16,4,7168]{2,1,0:T(4,128)(2,1)S(1)}, u32[]{:S(2)}, u32[]{:S(2)}) %all-to-all-start.3) | async-done | bytes 917536 | tf_op jit(solution)/shard_map/all_to_all | solution.py:60
  128.4 0.4 convert_reduce_fusion
  128.8 4.5 %fusion.1 = bf16[128,7168]{1,0:T(8,128)(2,1)} fusion(f32[4,7168]{1,0:T(4,128)S(1)} %convert_reduce_fusion, bf16[128,7168]{1,0:T(8,128)(2,1)} %param.8, s32[128]{0:T(128)S(1)} %sub.12, pred[128]{0:T(512)(128)(4,1)S(1)} %broadcast_compare_fusion.1), kind=kOutput, calls=%fused_computation.3 | convolution fusion | flops 46793728 | bytes 3785344 | tf_op jit(solution)/shard_map/dot_general | solution.py:100
  (11 shorter events, 0.1 us)
Async XLA Ops:
  0.6 37.5 %copy-start = (bf16[128,7168]{1,0:T(8,128)(2,1)S(1)}, bf16[128,7168]{1,0:T(8,128)(2,1)}, u32[]{:S(2)}) copy-start(bf16[128,7168]{1,0:T(8,128)(2,1)} %param.13) | copy-start | bytes 5505028
  35.5 2.1 %copy-start.2 = (bf16[7168,128]{1,0:T(8,128)(2,1)S(1)}, bf16[7168,128]{1,0:T(8,128)(2,1)}, u32[]{:S(2)}) copy-start(bf16[7168,128]{1,0:T(8,128)(2,1)} %param.12) | copy-start | bytes 5505028
  41.3 27.4 %copy-start.4 = (bf16[128,7168]{1,0:T(8,128)(2,1)S(1)}, bf16[128,7168]{1,0:T(8,128)(2,1)}, u32[]{:S(2)}) copy-start(bf16[128,7168]{1,0:T(8,128)(2,1)} %param.8) | copy-start | bytes 5505028
  97.5 2.1 %copy-start.1 = (bf16[7168,128]{1,0:T(8,128)(2,1)S(1)}, bf16[7168,128]{1,0:T(8,128)(2,1)}, u32[]{:S(2)}) copy-start(bf16[7168,128]{1,0:T(8,128)(2,1)} %param.11) | copy-start | bytes 5505028
  99.6 1.5 %copy-start.3 = (bf16[7168,128]{1,0:T(8,128)(2,1)S(1)}, bf16[7168,128]{1,0:T(8,128)(2,1)}, u32[]{:S(2)}) copy-start(bf16[7168,128]{1,0:T(8,128)(2,1)} %param.12) | copy-start | bytes 5505028
  103.1 25.3 %all-to-all-start.3 = ((bf16[16,4,7168]{2,1,0:T(4,128)(2,1)}), bf16[16,4,7168]{2,1,0:T(4,128)(2,1)S(1)}, u32[]{:S(2)}, u32[]{:S(2)}) async-start(bf16[16,4,7168]{2,1,0:T(4,128)(2,1)} %reshape.322), calls=%async_computation.3 | async-start | bytes 1835008 | tf_op jit(solution)/shard_map/all_to_all | solution.py:60
where the time goes:
time: 134 us; the launch traced here: 133 us
  blocking collectives  83.6 us (62%)
  matrix products  19.7 us (15%)
  waiting for transfers between devices  14.8 us (11%)
  local copies, waits for them, and re-layouts  7.2 us (5%)
  starting transfers between devices  4.47 us (3%)
  other arithmetic  2.74 us (2%)
    all_to_all x1, blocking collectives, local(): lax.all_to_all(spread(token_slots), 'expert', split_axis=0, concat_axis=0...  29.8 us
    all_to_all x1, blocking collectives, expert_section(): lax.all_to_all(out_rows, 'expert', split_axis=0, concat_axis=0, tiled=True)  27 us
    all_to_all x1, blocking collectives, local(): lax.all_to_all(spread(weighted_slots), 'expert', split_axis=0, concat_axi...  26.8 us
    all_to_all x1, waiting for transfers between devices, expert_section(): lax.all_to_all(input_rows, 'expert', split_axis=0, concat_axis=0, tiled=T...  14.8 us
    dot_general x1, matrix products, local(): jnp.dot(mixing, out_sum, precision=highest, preferred_element_type=jnp.fl...  5.45 us
    dot_general x1, matrix products, local(): jnp.dot(placement_flat, input_sum, precision=highest, preferred_element_t...  4.47 us
    all_to_all x1, starting transfers between devices, expert_section(): lax.all_to_all(input_rows, 'expert', split_axis=0, concat_axis=0, tiled=T...  4.47 us
  transfers between devices with their start and end apart: 1, of which 1 were waited for; matrix products, arithmetic and copies ran while one was open for 5% of the time, Pallas kernels for 0%

commit v1 on v0

v1 whole, which is shorter than its diff:
```python
import jax
import jax.numpy as jnp
from jax import lax
from jax.sharding import PartitionSpec as P

HID = 2048
PANEL = 128
CAP = 4
PANELS = HID // PANEL
AXIS = "expert"

f32 = jnp.float32
bf16 = jnp.bfloat16


def slot_tables(routes, gate_probs, experts):
    expert_ids = jnp.arange(experts, dtype=jnp.int32)
    matches = routes[:, :, None] == expert_ids[None, None, :]
    per_token = jnp.sum(matches.astype(jnp.int32), axis=1)
    slot_order = jnp.cumsum(per_token, axis=0) - per_token
    slot_ids = jnp.arange(CAP, dtype=jnp.int32)
    placement = (per_token[:, :, None] == 1) & (slot_order[:, :, None] == slot_ids[None, None, :])
    placement = placement.astype(f32)
    route_prob = jnp.sum(jnp.where(matches, gate_probs[:, :, None], 0.0), axis=1)
    slot_prob = jnp.sum(placement * route_prob[:, :, None], axis=0).reshape(-1)
    return (matches, placement, slot_prob)


def swap(x, offset):
    devices = lax.axis_size(AXIS)
    return lax.ppermute(x, AXIS, [(i, i ^ offset) for i in range(devices)])


def gather_rows(x):
    blocks = {0: x}
    for far in range(PANELS // 4 - 1, 0, -1):
        blocks[4 * far] = swap(x, 4 * far)
    for far in range(PANELS // 4):
        blocks[4 * far + 2] = swap(blocks[4 * far], 2)
    even = jnp.stack([blocks[k] for k in range(0, PANELS, 2)])
    return even, swap(even, 1)


def scatter_sum(even, odd):
    part = even.astype(f32) + swap(odd, 1).astype(f32)
    own = {}
    for far in range(PANELS // 4 - 1, -1, -1):
        own[far] = part[2 * far] + swap(part[2 * far + 1].astype(bf16), 2).astype(f32)
    total = own[0]
    for far in range(PANELS // 4 - 1, 0, -1):
        total = total + swap(own[far].astype(bf16), 4 * far).astype(f32)
    return total


def expert_compute(token_rows, grad_rows, w_gate, w_up, w_down):
    gate_pre = jnp.dot(token_rows, w_gate, preferred_element_type=f32)
    up_pre = jnp.dot(token_rows, w_up, preferred_element_type=f32)
    sigmoid_gate = jax.nn.sigmoid(gate_pre)
    silu_gate = gate_pre * sigmoid_gate
    hidden = (silu_gate * up_pre).astype(bf16)
    expert_out = jnp.dot(hidden, w_down, preferred_element_type=f32).astype(bf16)
    contract = (((1,), (1,)), ((), ()))
    hidden_grad = lax.dot_general(grad_rows, w_down, contract, preferred_element_type=f32)
    silu_slope = sigmoid_gate * (1.0 + gate_pre * (1.0 - sigmoid_gate))
    gate_grad = (hidden_grad * up_pre * silu_slope).astype(bf16)
    up_grad = (hidden_grad * silu_gate).astype(bf16)
    input_part = lax.dot_general(gate_grad, w_gate, contract, preferred_element_type=f32)
    input_part = input_part + lax.dot_general(up_grad, w_up, contract, preferred_element_type=f32)
    return (expert_out, input_part.astype(bf16))


def local(tokens, out_grad, routes, gate_probs, w_gate, w_up, w_down):
    devices = lax.axis_size(AXIS)
    experts = devices // PANELS
    tok_count, width = tokens.shape
    slot_total = experts * CAP
    matches, placement, slot_prob = slot_tables(routes, gate_probs, experts)
    placement_flat = placement.reshape(tok_count, slot_total)
    picker = placement_flat.T.astype(bf16)
    token_slots = jnp.dot(picker, tokens, preferred_element_type=f32).astype(bf16)
    grad_slots = jnp.dot(picker, out_grad, preferred_element_type=f32).astype(bf16)
    weighted_slots = (slot_prob[:, None] * grad_slots.astype(f32)).astype(bf16)

    send = jnp.concatenate(
        [token_slots.reshape(experts, CAP, width), weighted_slots.reshape(experts, CAP, width)], axis=1
    )
    rows = 2 * CAP * experts
    peers = [[e * PANELS + r for e in range(experts)] for r in range(PANELS)]
    if experts > 1:
        send = lax.all_to_all(send, AXIS, 0, 0, axis_index_groups=peers, tiled=True)
    even, odd = gather_rows(send.reshape(rows, width))
    everyone = jnp.stack([even, odd]).reshape(-1, 2, CAP, width)
    out_rows, input_rows = expert_compute(
        everyone[:, 0].reshape(-1, width), everyone[:, 1].reshape(-1, width), w_gate, w_up, w_down
    )
    back = jnp.stack([out_rows.reshape(-1, CAP, width), input_rows.reshape(-1, CAP, width)], axis=1)
    back = back.reshape(2, PANELS // 2, rows, width)
    total = scatter_sum(back[0], back[1]).reshape(experts, 2 * CAP, width)
    if experts > 1:
        total = lax.all_to_all(total, AXIS, 0, 0, axis_index_groups=peers, tiled=True)
    out_sum = total[:, :CAP].reshape(slot_total, width)
    input_sum = total[:, CAP:].reshape(slot_total, width)

    highest = lax.Precision.HIGHEST
    mixing = placement_flat * slot_prob[None, :]
    layer_moe = jnp.dot(mixing, out_sum, precision=highest, preferred_element_type=f32)
    layer_out = (tokens.astype(f32) + layer_moe).astype(bf16)
    input_moe = jnp.dot(placement_flat, input_sum, precision=highest, preferred_element_type=f32)
    input_grad = (out_grad.astype(f32) + input_moe).astype(bf16)
    slot_dot = jnp.sum(grad_slots.astype(f32) * out_sum, axis=1)
    token_dot = jnp.sum(placement * slot_dot.reshape(experts, CAP)[None, :, :], axis=2)
    prob_grad = jnp.sum(jnp.where(matches, token_dot[:, None, :], 0.0), axis=2)
    return (layer_out, input_grad, prob_grad)


def solution(mesh):
    rows = P(("groups", AXIS), None)
    return jax.shard_map(
        local,
        mesh=mesh,
        in_specs=(rows, rows, rows, rows, P(None, AXIS), P(None, AXIS), P(AXIS, None)),
        out_specs=(rows, rows, rows),
        check_vma=False,
    )
```

time: 134 us -> 94.9 us (0.71)
  blocking collectives: 83.6 us -> 0 us
  starting transfers between devices: 4.47 us -> 20.1 us
  waiting for transfers between devices: 14.8 us -> 27.1 us
  local copies, waits for them, and re-layouts: 7.2 us -> 19.2 us
  other arithmetic: 2.74 us -> 9.65 us
  matrix products: 19.7 us -> 17.5 us
    all_to_all x3 -> x0, blocking collectives: 83.6 us -> none  [the longest x1 29.8 us: local(): lax.all_to_all(spread(token_slots), 'expert', split_axis=0, concat_axis=0...]
    ppermute x0 -> x16, waiting for transfers between devices: none -> 27.1 us  [swap(): return lax.ppermute(x, AXIS, [(i, i ^ offset) for i in range(devices)])]
    ppermute x0 -> x16, starting transfers between devices: none -> 20.1 us  [swap(): return lax.ppermute(x, AXIS, [(i, i ^ offset) for i in range(devices)])]
    all_to_all x1 -> x0, waiting for transfers between devices: 14.8 us -> none  [expert_section(): lax.all_to_all(input_rows, 'expert', split_axis=0, concat_axis=0, tiled=T...]
    another operation x2 -> x5, other arithmetic: 0.27 us -> 7.48 us  [the longest x1 3.87 us: local(): jnp.stack([out_rows.reshape(-1, CAP, width), input_rows.reshape(-1, CAP,...]
    another operation x1 -> x6, local copies, waits for them, and re-layouts: 0.11 us -> 6.77 us  [the longest x2 3.86 us: local(): jnp.stack([out_rows.reshape(-1, CAP, width), input_rows.reshape(-1, CAP,...]
    all_to_all x1 -> x0, starting transfers between devices: 4.47 us -> none  [expert_section(): lax.all_to_all(input_rows, 'expert', split_axis=0, concat_axis=0, tiled=T...]
    slice x0 -> x1, local copies, waits for them, and re-layouts: none -> 3.01 us  [local(): everyone[:, 1].reshape(-1, width)]
  transfers between devices with their start and end apart: 1 -> 16, of which waited for: 1 -> 9; matrix products, arithmetic and copies ran while one was open for 5% -> 3% of each run, Pallas kernels for 0% -> 0%
where the time goes in v1:
time: 94.9 us; the launch traced here: 94.5 us
  waiting for transfers between devices  27.1 us (29%)
  starting transfers between devices  20.1 us (21%)
  local copies, waits for them, and re-layouts  19.2 us (20%)
  matrix products  17.5 us (18%)
  other arithmetic  9.65 us (10%)
    ppermute x16, waiting for transfers between devices, swap(): return lax.ppermute(x, AXIS, [(i, i ^ offset) for i in range(devices)])  27.1 us
    ppermute x16, starting transfers between devices, swap(): return lax.ppermute(x, AXIS, [(i, i ^ offset) for i in range(devices)])  20.1 us
    dot_general x1, matrix products, local(): jnp.dot(mixing, out_sum, precision=highest, preferred_element_type=f32)  4.45 us
    reshape x1, local copies, waits for them, and re-layouts, local(): everyone = jnp.stack([even, odd]).reshape(-1, 2, CAP, width)  4.04 us
    another operation x1, other arithmetic, local(): jnp.stack([out_rows.reshape(-1, CAP, width), input_rows.reshape(-1, CAP,...  3.87 us
    another operation x2, local copies, waits for them, and re-layouts, local(): jnp.stack([out_rows.reshape(-1, CAP, width), input_rows.reshape(-1, CAP,...  3.86 us
    slice x1, local copies, waits for them, and re-layouts, local(): everyone[:, 1].reshape(-1, width)  3.01 us
    dot_general x1, matrix products, local(): jnp.dot(placement_flat, input_sum, precision=highest, preferred_element_t...  3 us
  transfers between devices with their start and end apart: 16, of which 9 were waited for; matrix products, arithmetic and copies ran while one was open for 3% of the time, Pallas kernels for 0%

profile of v1, /device:TPU:0, one launch (start us, length us, event | category | flops | bytes accessed | tf_op | source)
XLA Modules:
  0.0 94.5 jit_solution(13871125978832934967)
XLA Ops:
  2.1 2.0 %fusion.4 = bf16[1,4,7168]{2,1,0:T(4,128)(2,1)S(1)} fusion(bf16[128,7168]{1,0:T(8,128)(2,1)} %param.7, s32[128]{0:T(128)S(1)} %sub.12, pred[128]{0:T(512)(128)(4,1)S(1)} %broadcast_compare_fusion.1), kind=kOutput, calls=%fused_computation.10 | convolution fusion | flops 7370752 | bytes 1892992 | tf_op jit(solution)/shard_map/dot_general | solution.py:80
  4.5 5.1 %collective-permute-start.5 = (bf16[8,7168]{1,0:T(8,128)(2,1)S(1)}, bf16[8,7168]{1,0:T(8,128)(2,1)S(1)}, u32[]{:S(2)}, u32[]{:S(2)}) collective-permute-start(bf16[8,7168]{1,0:T(8,128)(2,1)S(1)} %get-tuple-element.18), channel_id=1, source_target_pairs={{0,12},{1,13},{2,14},{3,15},{4,8},{5,9},{6,10},{7,11},{8,4},{9,5},... | collective-permute-start | bytes 344072 | tf_op jit(solution)/shard_map/ppermute | solution.py:31
  10.3 1.7 %collective-permute-start = (bf16[8,7168]{1,0:T(8,128)(2,1)S(1)}, bf16[8,7168]{1,0:T(8,128)(2,1)S(1)}, u32[]{:S(2)}, u32[]{:S(2)}) collective-permute-start(bf16[8,7168]{1,0:T(8,128)(2,1)S(1)} %get-tuple-element.18), channel_id=1, source_target_pairs={{0,2},{1,3},{2,0},{3,1},{4,6},{5,7},{6,4},{7,5},{8,10},{9,11},{10,... | collective-permute-start | bytes 344072 | tf_op jit(solution)/shard_map/ppermute | solution.py:31
  12.0 1.8 %collective-permute-done.5 = bf16[8,7168]{1,0:T(8,128)(2,1)S(1)} collective-permute-done((bf16[8,7168]{1,0:T(8,128)(2,1)S(1)}, bf16[8,7168]{1,0:T(8,128)(2,1)S(1)}, u32[]{:S(2)}, u32[]{:S(2)}) %collective-permute-start.5) | collective-permute-done | bytes 114720 | tf_op jit(solution)/shard_map/ppermute | solution.py:31
  13.7 1.7 %collective-permute-start.6 = (bf16[8,7168]{1,0:T(8,128)(2,1)S(1)}, bf16[8,7168]{1,0:T(8,128)(2,1)S(1)}, u32[]{:S(2)}, u32[]{:S(2)}) collective-permute-start(bf16[8,7168]{1,0:T(8,128)(2,1)S(1)} %collective-permute-done.5), channel_id=1, source_target_pairs={{0,2},{1,3},{2,0},{3,1},{4,6},{5,7},{6,4},{7,5},{8,10},{9,11},{10,... | collective-permute-start | bytes 344072 | tf_op jit(solution)/shard_map/ppermute | solution.py:31
  15.5 3.9 %collective-permute-done.3 = bf16[8,7168]{1,0:T(8,128)(2,1)S(1)} collective-permute-done((bf16[8,7168]{1,0:T(8,128)(2,1)S(1)}, bf16[8,7168]{1,0:T(8,128)(2,1)S(1)}, u32[]{:S(2)}, u32[]{:S(2)}) %collective-permute-start.3) | collective-permute-done | bytes 114720 | tf_op jit(solution)/shard_map/ppermute | solution.py:31
  19.3 1.5 %collective-permute-start.4 = (bf16[8,7168]{1,0:T(8,128)(2,1)S(1)}, bf16[8,7168]{1,0:T(8,128)(2,1)S(1)}, u32[]{:S(2)}, u32[]{:S(2)}) collective-permute-start(bf16[8,7168]{1,0:T(8,128)(2,1)S(1)} %collective-permute-done.3), channel_id=1, source_target_pairs={{0,2},{1,3},{2,0},{3,1},{4,6},{5,7},{6,4},{7,5},{8,10},{9,11},{10,... | collective-permute-start | bytes 344072 | tf_op jit(solution)/shard_map/ppermute | solution.py:31
  21.4 4.6 %collective-permute-done.2 = bf16[8,7168]{1,0:T(8,128)(2,1)S(1)} collective-permute-done((bf16[8,7168]{1,0:T(8,128)(2,1)S(1)}, bf16[8,7168]{1,0:T(8,128)(2,1)S(1)}, u32[]{:S(2)}, u32[]{:S(2)}) %collective-permute-start.2) | collective-permute-done | bytes 114720 | tf_op jit(solution)/shard_map/ppermute | solution.py:31
  26.2 2.5 %collective-permute-done.7 = bf16[8,8,7168]{2,1,0:T(8,128)(2,1)S(1)} collective-permute-done((bf16[8,8,7168]{2,1,0:T(8,128)(2,1)S(1)}, bf16[8,8,7168]{2,1,0:T(8,128)(2,1)S(1)}, u32[]{:S(2)}, u32[]{:S(2)}) %collective-permute-start.7) | collective-permute-done | bytes 917536 | tf_op jit(solution)/shard_map/ppermute | solution.py:31
  28.6 1.4 %pad_maximum_fusion = bf16[2,8,8,7168]{3,2,1,0:T(8,128)(2,1)} fusion(bf16[1,8,8,7168]{3,2,1,0:T(8,128)(2,1)S(1)} %bitcast.95, bf16[1,8,8,7168]{3,2,1,0:T(8,128)(2,1)S(1)} %bitcast.94), kind=kLoop, calls=%fused_computation.11 | loop fusion | flops 917504 | bytes 3670016 | tf_op jit(solution)/shard_map/stack | solution.py:92
  30.0 4.0 %reshape.375 = bf16[16,2,4,7168]{3,2,1,0:T(4,128)(2,1)} reshape(bf16[2,8,8,7168]{3,2,1,0:T(8,128)(2,1)} %pad_maximum_fusion) | data formatting | bytes 3670016 | tf_op jit(solution)/shard_map/reshape | solution.py:92
  34.1 3.0 %fusion.49 = (bf16[16,1,4,7168]{3,2,1,0:T(4,128)(2,1)S(1)}, bf16[16,1,4,7168]{3,2,1,0:T(4,128)(2,1)}) fusion(bf16[16,2,4,7168]{3,2,1,0:T(4,128)(2,1)} %reshape.375), kind=kLoop, calls=%fused_computation.91 | loop fusion | bytes 3670016 | tf_op jit(solution)/shard_map/slice | solution.py:94
  38.2 1.7 %reshape_squeeze.6 = bf16[64,7168]{1,0:T(8,128)(2,1)S(1)} reshape(bf16[16,1,4,7168]{3,2,1,0:T(4,128)(2,1)} %get-tuple-element.13) | data formatting | bytes 1835008 | tf_op jit(solution)/shard_map/reshape;squeeze | solution.py:94
  39.9 2.1 %fusion.50 = f32[64,128]{1,0:T(8,128)S(1)} fusion(bf16[64,7168]{1,0:T(8,128)(2,1)S(1)} %reshape_squeeze.6, bf16[7168,128]{1,0:T(8,128)(2,1)} %param.11), kind=kOutput, calls=%fused_computation.92 | convolution fusion | flops 117440512 | bytes 2785280 | tf_op jit(solution)/shard_map/dot_general | solution.py:56
  45.6 2.4 %fusion.22 = f32[64,7168]{1,0:T(8,128)S(1)} fusion(bf16[7168,128]{1,0:T(8,128)(2,1)} %param.11, f32[64,128]{1,0:T(8,128)S(1)} %fusion.50, f32[64,128]{1,0:T(8,128)S(1)} %fusion.52, f32[64,128]{1,0:T(8,128)S(1)} %fusion.51), kind=kOutput, calls=%fused_computation.57 | convolution fusion | flops 117522432 | bytes 3768320 | tf_op jit(solution)/shard_map/dot_general | solution.py:67
  48.0 1.7 %fusion.2 = bf16[64,7168]{1,0:T(8,128)(2,1)} fusion(f32[64,7168]{1,0:T(8,128)S(1)} %fusion.22, bf16[7168,128]{1,0:T(8,128)(2,1)S(1)} %copy-done.3, f32[64,128]{1,0:T(8,128)S(1)} %fusion.52, f32[64,128]{1,0:T(8,128)S(1)} %fusion.50), kind=kOutput, calls=%fused_computation.6 | convolution fusion | flops 118407168 | bytes 4653056 | tf_op jit(solution)/shard_map/dot_general | solution.py:68
  49.7 2.6 %stack_reshape.7 = bf16[16,1,4,7168]{3,2,0,1:T(4,128)(2,1)} reshape(bf16[64,7168]{1,0:T(8,128)(2,1)} %fusion.2) | data formatting | bytes 1835008 | tf_op jit(solution)/shard_map/stack;reshape | solution.py:96
  52.3 3.9 %pad_maximum_fusion.1 = (bf16[8,2,4,7168]{3,2,1,0:T(4,128)(2,1)}, f32[8,2,4,7168]{3,2,1,0:T(4,128)}) fusion(bf16[16,1,4,7168]{3,2,1,0:T(4,128)(2,1)} %bitcast.93, bf16[16,1,4,7168]{3,2,1,0:T(4,128)(2,1)S(1)} %bitcast.92), kind=kLoop, calls=%fused_computation.17 | loop fusion | flops 1376256 | bytes 4587520 | tf_op jit(solution)/shard_map/stack | solution.py:96
  56.2 1.7 %squeeze.20 = bf16[8,8,7168]{2,1,0:T(8,128)(2,1)S(1)} reshape(bf16[8,2,4,7168]{3,2,1,0:T(4,128)(2,1)} %get-tuple-element.10) | data formatting | bytes 1835008 | tf_op jit(solution)/shard_map/squeeze | solution.py:98
  58.0 2.9 %reshape.379 = f32[8,8,7168]{2,1,0:T(8,128)} reshape(f32[8,2,4,7168]{3,2,1,0:T(4,128)} %get-tuple-element.11) | data formatting | bytes 3670016 | tf_op jit(solution)/shard_map/convert_element_type | solution.py:45
  60.9 2.0 %fusion.48 = (bf16[8,8,7168]{2,1,0:T(8,128)(2,1)S(1)}, f32[8,8,7168]{2,1,0:T(8,128)S(1)}) fusion(f32[8,8,7168]{2,1,0:T(8,128)} %reshape.379, bf16[8,8,7168]{2,1,0:T(8,128)(2,1)} %collective-permute-done.8), kind=kLoop, calls=%fused_computation.90 | loop fusion | flops 1376256 | bytes 5505024 | tf_op jit(solution)/shard_map/convert.4
  62.9 1.6 %collective-permute-start.14 = (bf16[8,7168]{1,0:T(8,128)(2,1)S(1)}, bf16[8,7168]{1,0:T(8,128)(2,1)S(1)}, u32[]{:S(2)}, u32[]{:S(2)}) collective-permute-start(bf16[8,7168]{1,0:T(8,128)(2,1)S(1)} %get-tuple-element.15), channel_id=1, source_target_pairs={{0,2},{1,3},{2,0},{3,1},{4,6},{5,7},{6,4},{7,5},{8,10},{9,11},{10,... | collective-permute-start | bytes 344072 | tf_op jit(solution)/shard_map/ppermute | solution.py:31
  65.0 1.5 %collective-permute-start.10 = (bf16[8,7168]{1,0:T(8,128)(2,1)S(1)}, bf16[8,7168]{1,0:T(8,128)(2,1)S(1)}, u32[]{:S(2)}, u32[]{:S(2)}) collective-permute-start(bf16[8,7168]{1,0:T(8,128)(2,1)S(1)} %get-tuple-element.17), channel_id=1, source_target_pairs={{0,2},{1,3},{2,0},{3,1},{4,6},{5,7},{6,4},{7,5},{8,10},{9,11},{10,... | collective-permute-start | bytes 344072 | tf_op jit(solution)/shard_map/ppermute | solution.py:31
  67.1 1.9 %collective-permute-done.14 = bf16[8,7168]{1,0:T(8,128)(2,1)S(1)} collective-permute-done((bf16[8,7168]{1,0:T(8,128)(2,1)S(1)}, bf16[8,7168]{1,0:T(8,128)(2,1)S(1)}, u32[]{:S(2)}, u32[]{:S(2)}) %collective-permute-start.14) | collective-permute-done | bytes 114720 | tf_op jit(solution)/shard_map/ppermute | solution.py:31
  69.0 2.5 %collective-permute-done.12 = bf16[8,7168]{1,0:T(8,128)(2,1)S(1)} collective-permute-done((bf16[8,7168]{1,0:T(8,128)(2,1)S(1)}, bf16[8,7168]{1,0:T(8,128)(2,1)S(1)}, u32[]{:S(2)}, u32[]{:S(2)}) %collective-permute-start.12) | collective-permute-done | bytes 114720 | tf_op jit(solution)/shard_map/ppermute | solution.py:31
  71.4 2.5 %collective-permute-done.10 = bf16[8,7168]{1,0:T(8,128)(2,1)S(1)} collective-permute-done((bf16[8,7168]{1,0:T(8,128)(2,1)S(1)}, bf16[8,7168]{1,0:T(8,128)(2,1)S(1)}, u32[]{:S(2)}, u32[]{:S(2)}) %collective-permute-start.10) | collective-permute-done | bytes 114720 | tf_op jit(solution)/shard_map/ppermute | solution.py:31
  74.0 2.3 %collective-permute-start.11 = (bf16[8,7168]{1,0:T(8,128)(2,1)S(1)}, bf16[8,7168]{1,0:T(8,128)(2,1)S(1)}, u32[]{:S(2)}, u32[]{:S(2)}) collective-permute-start(bf16[8,7168]{1,0:T(8,128)(2,1)S(1)} %get-tuple-element.7), channel_id=1, source_target_pairs={{0,12},{1,13},{2,14},{3,15},{4,8},{5,9},{6,10},{7,11},{8,4},{9,5},... | collective-permute-start | bytes 344072 | tf_op jit(solution)/shard_map/ppermute | solution.py:31
  76.3 2.1 %collective-permute-start.15 = (bf16[8,7168]{1,0:T(8,128)(2,1)S(1)}, bf16[8,7168]{1,0:T(8,128)(2,1)S(1)}, u32[]{:S(2)}, u32[]{:S(2)}) collective-permute-start(bf16[8,7168]{1,0:T(8,128)(2,1)S(1)} %get-tuple-element.9), channel_id=1, source_target_pairs={{0,4},{1,5},{2,6},{3,7},{4,0},{5,1},{6,2},{7,3},{8,12},{9,13},{10,... | collective-permute-start | bytes 344072 | tf_op jit(solution)/shard_map/ppermute | solution.py:31
  78.4 3.5 %collective-permute-done.11 = bf16[8,7168]{1,0:T(8,128)(2,1)S(1)} collective-permute-done((bf16[8,7168]{1,0:T(8,128)(2,1)S(1)}, bf16[8,7168]{1,0:T(8,128)(2,1)S(1)}, u32[]{:S(2)}, u32[]{:S(2)}) %collective-permute-start.11) | collective-permute-done | bytes 114720 | tf_op jit(solution)/shard_map/ppermute | solution.py:31
  81.9 4.1 %collective-permute-done.13 = bf16[8,7168]{1,0:T(8,128)(2,1)S(1)} collective-permute-done((bf16[8,7168]{1,0:T(8,128)(2,1)S(1)}, bf16[8,7168]{1,0:T(8,128)(2,1)S(1)}, u32[]{:S(2)}, u32[]{:S(2)}) %collective-permute-start.13) | collective-permute-done | bytes 114720 | tf_op jit(solution)/shard_map/ppermute | solution.py:31
  86.3 4.4 %fusion = bf16[128,7168]{1,0:T(8,128)(2,1)} fusion(bf16[128,7168]{1,0:T(8,128)(2,1)S(1)} %copy-done.1, f32[1,8,7168]{2,1,0:T(8,128)S(1)} %fusion.17, f32[4]{0:T(128)S(1)} %select_reduce_fusion.2, s32[128]{0:T(128)S(1)} %sub.12, pred[128]{0:T(512)(128)(4,1)S(1)} %broadcast_compare_fusion.1), kind=kOutput, calls=%fused_computation.2 | convolution fusion | flops 46794240 | bytes 3786240 | tf_op jit(solution)/shard_map/dot_general | solution.py:106
  90.8 3.0 %fusion.1 = bf16[128,7168]{1,0:T(8,128)(2,1)} fusion(bf16[128,7168]{1,0:T(8,128)(2,1)S(1)} %copy-done.5, f32[1,8,7168]{2,1,0:T(8,128)S(1)} %fusion.17, s32[128]{0:T(128)S(1)} %sub.12, pred[128]{0:T(512)(128)(4,1)S(1)} %broadcast_compare_fusion.1), kind=kOutput, calls=%fused_computation.3 | convolution fusion | flops 46793728 | bytes 3785728 | tf_op jit(solution)/shard_map/dot_general | solution.py:108
  (60 shorter events, 10.3 us)
Async XLA Ops:
  0.6 41.8 %copy-start = (bf16[128,7168]{1,0:T(8,128)(2,1)S(1)}, bf16[128,7168]{1,0:T(8,128)(2,1)}, u32[]{:S(2)}) copy-start(bf16[128,7168]{1,0:T(8,128)(2,1)} %param.13) | copy-start | bytes 5505028
  1.9 2.1 %copy-start.4 = (bf16[128,7168]{1,0:T(8,128)(2,1)S(1)}, bf16[128,7168]{1,0:T(8,128)(2,1)}, u32[]{:S(2)}) copy-start(bf16[128,7168]{1,0:T(8,128)(2,1)} %param.8) | copy-start | bytes 5505028
  4.5 9.2 %collective-permute-start.5 = (bf16[8,7168]{1,0:T(8,128)(2,1)S(1)}, bf16[8,7168]{1,0:T(8,128)(2,1)S(1)}, u32[]{:S(2)}, u32[]{:S(2)}) collective-permute-start(bf16[8,7168]{1,0:T(8,128)(2,1)S(1)} %get-tuple-element.18), channel_id=1, source_target_pairs={{0,12},{1,13},{2,14},{3,15},{4,8},{5,9},{6,10},{7,11},{8,4},{9,5},... | collective-permute-start | bytes 344072 | tf_op jit(solution)/shard_map/ppermute | solution.py:31
  9.7 9.7 %collective-permute-start.3 = (bf16[8,7168]{1,0:T(8,128)(2,1)S(1)}, bf16[8,7168]{1,0:T(8,128)(2,1)S(1)}, u32[]{:S(2)}, u32[]{:S(2)}) collective-permute-start(bf16[8,7168]{1,0:T(8,128)(2,1)S(1)} %get-tuple-element.18), channel_id=1, source_target_pairs={{0,8},{1,9},{2,10},{3,11},{4,12},{5,13},{6,14},{7,15},{8,0},{9,1},... | collective-permute-start | bytes 344072 | tf_op jit(solution)/shard_map/ppermute | solution.py:31
  9.7 11.2 %collective-permute-start.1 = (bf16[8,7168]{1,0:T(8,128)(2,1)S(1)}, bf16[8,7168]{1,0:T(8,128)(2,1)S(1)}, u32[]{:S(2)}, u32[]{:S(2)}) collective-permute-start(bf16[8,7168]{1,0:T(8,128)(2,1)S(1)} %get-tuple-element.18), channel_id=1, source_target_pairs={{0,4},{1,5},{2,6},{3,7},{4,0},{5,1},{6,2},{7,3},{8,12},{9,13},{10,... | collective-permute-start | bytes 344072 | tf_op jit(solution)/shard_map/ppermute | solution.py:31
  10.3 11.1 %collective-permute-start = (bf16[8,7168]{1,0:T(8,128)(2,1)S(1)}, bf16[8,7168]{1,0:T(8,128)(2,1)S(1)}, u32[]{:S(2)}, u32[]{:S(2)}) collective-permute-start(bf16[8,7168]{1,0:T(8,128)(2,1)S(1)} %get-tuple-element.18), channel_id=1, source_target_pairs={{0,2},{1,3},{2,0},{3,1},{4,6},{5,7},{6,4},{7,5},{8,10},{9,11},{10,... | collective-permute-start | bytes 344072 | tf_op jit(solution)/shard_map/ppermute | solution.py:31
  13.7 12.3 %collective-permute-start.6 = (bf16[8,7168]{1,0:T(8,128)(2,1)S(1)}, bf16[8,7168]{1,0:T(8,128)(2,1)S(1)}, u32[]{:S(2)}, u32[]{:S(2)}) collective-permute-start(bf16[8,7168]{1,0:T(8,128)(2,1)S(1)} %collective-permute-done.5), channel_id=1, source_target_pairs={{0,2},{1,3},{2,0},{3,1},{4,6},{5,7},{6,4},{7,5},{8,10},{9,11},{10,... | collective-permute-start | bytes 344072 | tf_op jit(solution)/shard_map/ppermute | solution.py:31
  19.3 6.7 %collective-permute-start.4 = (bf16[8,7168]{1,0:T(8,128)(2,1)S(1)}, bf16[8,7168]{1,0:T(8,128)(2,1)S(1)}, u32[]{:S(2)}, u32[]{:S(2)}) collective-permute-start(bf16[8,7168]{1,0:T(8,128)(2,1)S(1)} %collective-permute-done.3), channel_id=1, source_target_pairs={{0,2},{1,3},{2,0},{3,1},{4,6},{5,7},{6,4},{7,5},{8,10},{9,11},{10,... | collective-permute-start | bytes 344072 | tf_op jit(solution)/shard_map/ppermute | solution.py:31
  20.8 5.2 %collective-permute-start.2 = (bf16[8,7168]{1,0:T(8,128)(2,1)S(1)}, bf16[8,7168]{1,0:T(8,128)(2,1)S(1)}, u32[]{:S(2)}, u32[]{:S(2)}) collective-permute-start(bf16[8,7168]{1,0:T(8,128)(2,1)S(1)} %collective-permute-done.1), channel_id=1, source_target_pairs={{0,2},{1,3},{2,0},{3,1},{4,6},{5,7},{6,4},{7,5},{8,10},{9,11},{10,... | collective-permute-start | bytes 344072 | tf_op jit(solution)/shard_map/ppermute | solution.py:31
  26.1 2.5 %collective-permute-start.7 = (bf16[8,8,7168]{2,1,0:T(8,128)(2,1)S(1)}, bf16[8,8,7168]{2,1,0:T(8,128)(2,1)S(1)}, u32[]{:S(2)}, u32[]{:S(2)}) collective-permute-start(bf16[8,8,7168]{2,1,0:T(8,128)(2,1)S(1)} %bitcast_dynamic-update-slice_fusion), channel_id=1, source_target_pairs={{0,1},{1,0},{2,3},{3,2},{4,5},{5,4},{6,7},{7,6},{8,9},{9,8},{10,11... | collective-permute-start | bytes 2752520 | tf_op jit(solution)/shard_map/ppermute | solution.py:31
  39.9 2.1 %copy-start.2 = (bf16[7168,128]{1,0:T(8,128)(2,1)S(1)}, bf16[7168,128]{1,0:T(8,128)(2,1)}, u32[]{:S(2)}) copy-start(bf16[7168,128]{1,0:T(8,128)(2,1)} %param.12) | copy-start | bytes 5505028
  42.0 1.2 %copy-start.7 = (bf16[64,7168]{1,0:T(8,128)(2,1)S(1)}, bf16[64,7168]{1,0:T(8,128)(2,1)}, u32[]{:S(2)}) copy-start(bf16[64,7168]{1,0:T(8,128)(2,1)} %reshape_squeeze.7) | copy-start | bytes 2752516
  45.6 2.4 %copy-start.3 = (bf16[7168,128]{1,0:T(8,128)(2,1)S(1)}, bf16[7168,128]{1,0:T(8,128)(2,1)}, u32[]{:S(2)}) copy-start(bf16[7168,128]{1,0:T(8,128)(2,1)} %param.12) | copy-start | bytes 5505028
  49.7 2.6 %copy-start.6 = (bf16[16,1,4,7168]{3,2,0,1:T(4,128)(2,1)S(1)}, bf16[16,1,4,7168]{3,2,0,1:T(4,128)(2,1)}, u32[]{:S(2)}) copy-start(bf16[16,1,4,7168]{3,2,0,1:T(4,128)(2,1)} %stack_reshape.6) | copy-start | bytes 2752516
  57.8 3.1 %collective-permute-start.8 = (bf16[8,8,7168]{2,1,0:T(8,128)(2,1)S(1)}, bf16[8,8,7168]{2,1,0:T(8,128)(2,1)}, u32[]{:S(2)}, u32[]{:S(2)}) collective-permute-start(bf16[8,8,7168]{2,1,0:T(8,128)(2,1)S(1)} %squeeze.20), channel_id=1, source_target_pairs={{0,1},{1,0},{2,3},{3,2},{4,5},{5,4},{6,7},{7,6},{8,9},{9,8},{10,11... | collective-permute-start | bytes 2752520 | tf_op jit(solution)/shard_map/ppermute | solution.py:31
  62.9 23.4 %copy-start.1 = (bf16[128,7168]{1,0:T(8,128)(2,1)S(1)}, bf16[128,7168]{1,0:T(8,128)(2,1)}, u32[]{:S(2)}) copy-start(bf16[128,7168]{1,0:T(8,128)(2,1)} %param.7) | copy-start | bytes 5505028
  62.9 6.1 %collective-permute-start.14 = (bf16[8,7168]{1,0:T(8,128)(2,1)S(1)}, bf16[8,7168]{1,0:T(8,128)(2,1)S(1)}, u32[]{:S(2)}, u32[]{:S(2)}) collective-permute-start(bf16[8,7168]{1,0:T(8,128)(2,1)S(1)} %get-tuple-element.15), channel_id=1, source_target_pairs={{0,2},{1,3},{2,0},{3,1},{4,6},{5,7},{6,4},{7,5},{8,10},{9,11},{10,... | collective-permute-start | bytes 344072 | tf_op jit(solution)/shard_map/ppermute | solution.py:31
  64.5 6.9 %collective-permute-start.12 = (bf16[8,7168]{1,0:T(8,128)(2,1)S(1)}, bf16[8,7168]{1,0:T(8,128)(2,1)S(1)}, u32[]{:S(2)}, u32[]{:S(2)}) collective-permute-start(bf16[8,7168]{1,0:T(8,128)(2,1)S(1)} %get-tuple-element.16), channel_id=1, source_target_pairs={{0,2},{1,3},{2,0},{3,1},{4,6},{5,7},{6,4},{7,5},{8,10},{9,11},{10,... | collective-permute-start | bytes 344072 | tf_op jit(solution)/shard_map/ppermute | solution.py:31
  65.0 8.8 %collective-permute-start.10 = (bf16[8,7168]{1,0:T(8,128)(2,1)S(1)}, bf16[8,7168]{1,0:T(8,128)(2,1)S(1)}, u32[]{:S(2)}, u32[]{:S(2)}) collective-permute-start(bf16[8,7168]{1,0:T(8,128)(2,1)S(1)} %get-tuple-element.17), channel_id=1, source_target_pairs={{0,2},{1,3},{2,0},{3,1},{4,6},{5,7},{6,4},{7,5},{8,10},{9,11},{10,... | collective-permute-start | bytes 344072 | tf_op jit(solution)/shard_map/ppermute | solution.py:31
  66.6 11.9 %collective-permute-start.9 = (bf16[8,7168]{1,0:T(8,128)(2,1)S(1)}, bf16[8,7168]{1,0:T(8,128)(2,1)S(1)}, u32[]{:S(2)}, u32[]{:S(2)}) collective-permute-start(bf16[8,7168]{1,0:T(8,128)(2,1)S(1)} %get-tuple-element.14), channel_id=1, source_target_pairs={{0,2},{1,3},{2,0},{3,1},{4,6},{5,7},{6,4},{7,5},{8,10},{9,11},{10,... | collective-permute-start | bytes 344072 | tf_op jit(solution)/shard_map/ppermute | solution.py:31
  74.0 8.0 %collective-permute-start.11 = (bf16[8,7168]{1,0:T(8,128)(2,1)S(1)}, bf16[8,7168]{1,0:T(8,128)(2,1)S(1)}, u32[]{:S(2)}, u32[]{:S(2)}) collective-permute-start(bf16[8,7168]{1,0:T(8,128)(2,1)S(1)} %get-tuple-element.7), channel_id=1, source_target_pairs={{0,12},{1,13},{2,14},{3,15},{4,8},{5,9},{6,10},{7,11},{8,4},{9,5},... | collective-permute-start | bytes 344072 | tf_op jit(solution)/shard_map/ppermute | solution.py:31
  76.3 9.7 %collective-permute-start.13 = (bf16[8,7168]{1,0:T(8,128)(2,1)S(1)}, bf16[8,7168]{1,0:T(8,128)(2,1)S(1)}, u32[]{:S(2)}, u32[]{:S(2)}) collective-permute-start(bf16[8,7168]{1,0:T(8,128)(2,1)S(1)} %get-tuple-element.8), channel_id=1, source_target_pairs={{0,8},{1,9},{2,10},{3,11},{4,12},{5,13},{6,14},{7,15},{8,0},{9,1},... | collective-permute-start | bytes 344072 | tf_op jit(solution)/shard_map/ppermute | solution.py:31
  76.3 9.7 %collective-permute-start.15 = (bf16[8,7168]{1,0:T(8,128)(2,1)S(1)}, bf16[8,7168]{1,0:T(8,128)(2,1)S(1)}, u32[]{:S(2)}, u32[]{:S(2)}) collective-permute-start(bf16[8,7168]{1,0:T(8,128)(2,1)S(1)} %get-tuple-element.9), channel_id=1, source_target_pairs={{0,4},{1,5},{2,6},{3,7},{4,0},{5,1},{6,2},{7,3},{8,12},{9,13},{10,... | collective-permute-start | bytes 344072 | tf_op jit(solution)/shard_map/ppermute | solution.py:31
  86.3 4.5 %copy-start.5 = (bf16[128,7168]{1,0:T(8,128)(2,1)S(1)}, bf16[128,7168]{1,0:T(8,128)(2,1)}, u32[]{:S(2)}) copy-start(bf16[128,7168]{1,0:T(8,128)(2,1)} %param.8) | copy-start | bytes 5505028

commit v2 on v1

v2 whole, which is shorter than its diff:
```python
import functools

import jax
import jax.numpy as jnp
from jax import lax
from jax.experimental import pallas as pl
from jax.experimental.pallas import tpu as pltpu
from jax.sharding import PartitionSpec as P

HID = 2048
PANEL = 128
CAP = 4
PANELS = HID // PANEL
PAIR = 2 * CAP
AXIS = "expert"
MIB = 1 << 20

f32 = jnp.float32
bf16 = jnp.bfloat16
NT = (((1,), (1,)), ((), ()))
TN = (((0,), (0,)), ((), ()))


def chunk_of(width, most):
    return max(c for c in range(128, most + 1, 128) if width % c == 0)


def swap(x, offset):
    devices = lax.axis_size(AXIS)
    return lax.ppermute(x, AXIS, [(i, i ^ offset) for i in range(devices)])


def gather_rows(x):
    blocks = {0: x}
    for far in range(PANELS // 4 - 1, 0, -1):
        blocks[4 * far] = swap(x, 4 * far)
    for far in range(PANELS // 4):
        blocks[4 * far + 2] = swap(blocks[4 * far], 2)
    even = jnp.concatenate([blocks[k] for k in range(0, PANELS, 2)], axis=0)
    return even, swap(even, 1)


def scatter_sum(even, odd):
    rows = even.shape[0] // (PANELS // 2)
    part = (even.astype(f32) + swap(odd, 1).astype(f32)).reshape(PANELS // 2, rows, -1)
    own = {}
    for far in range(PANELS // 4 - 1, -1, -1):
        own[far] = part[2 * far] + swap(part[2 * far + 1].astype(bf16), 2).astype(f32)
    terms = [own[0]]
    for far in range(PANELS // 4 - 1, 0, -1):
        terms.append(swap(own[far].astype(bf16), 4 * far))
    return terms


def slot_places(routes, expert):
    tokens = routes.shape[1]
    matches = routes == expert
    hit = jnp.max(jnp.where(matches, 1.0, 0.0), axis=0, keepdims=True)
    earlier = lax.broadcasted_iota(jnp.int32, (tokens, tokens), 0) < lax.broadcasted_iota(
        jnp.int32, (tokens, tokens), 1
    )
    hits = jnp.broadcast_to(hit, (PAIR, tokens)).astype(bf16)
    order = jnp.dot(hits, jnp.where(earlier, 1.0, 0.0).astype(bf16), preferred_element_type=f32)
    slot = lax.broadcasted_iota(jnp.int32, (PAIR, tokens), 0) % CAP
    place = jnp.where((hit > 0.5) & (order.astype(jnp.int32) == slot), 1.0, 0.0)
    return matches, place


def slot_probs(matches, place, probs):
    route_prob = jnp.sum(jnp.where(matches, probs, 0.0), axis=0, keepdims=True)
    return jnp.sum(place * route_prob, axis=1, keepdims=True)


def pick_kernel(experts, routes_ref, probs_ref, tokens_ref, grads_ref, send_ref, place_ref, weight_ref):
    @pl.when(pl.program_id(0) == 0)
    def _():
        for e in range(experts):
            matches, place = slot_places(routes_ref[...], e)
            place_ref[e] = place.astype(bf16)
            weight_ref[e] = slot_probs(matches, place, probs_ref[...])

    for e in range(experts):
        place = place_ref[e]
        picked = jnp.dot(place, tokens_ref[...], preferred_element_type=f32)
        grads = jnp.dot(place, grads_ref[...], preferred_element_type=f32)
        is_token = lax.broadcasted_iota(jnp.int32, picked.shape, 0) < CAP
        send_ref[e] = jnp.where(is_token, picked, weight_ref[e] * grads).astype(bf16)


def pick(routes, probs, tokens, grads, experts):
    count, width = tokens.shape
    chunk = chunk_of(width, 1792)
    topk = routes.shape[0]
    whole = lambda i: (0, 0)
    return pl.pallas_call(
        functools.partial(pick_kernel, experts),
        grid=(width // chunk,),
        in_specs=[
            pl.BlockSpec((topk, count), whole),
            pl.BlockSpec((topk, count), whole),
            pl.BlockSpec((count, chunk), lambda i: (0, i)),
            pl.BlockSpec((count, chunk), lambda i: (0, i)),
        ],
        out_specs=pl.BlockSpec((experts, PAIR, chunk), lambda i: (0, 0, i)),
        out_shape=jax.ShapeDtypeStruct((experts, PAIR, width), bf16),
        scratch_shapes=[pltpu.VMEM((experts, PAIR, count), bf16), pltpu.VMEM((experts, PAIR, 1), f32)],
        compiler_params=pltpu.CompilerParams(vmem_limit_bytes=16 * MIB),
        cost_estimate=pl.CostEstimate(
            flops=4 * experts * PAIR * count * width, bytes_accessed=4 * count * width, transcendentals=0
        ),
        name="pick_rows",
    )(routes, probs, tokens, grads)


def expert_kernel(chunk, even_ref, odd_ref, gate_ref, up_ref, down_ref, even_out, odd_out):
    half, width = even_ref.shape
    count = 2 * half
    units = down_ref.shape[0]
    gate_pre = jnp.zeros((count, units), f32)
    up_pre = jnp.zeros((count, units), f32)
    hidden_grad = jnp.zeros((count, units), f32)
    for start in range(0, width, chunk):
        cols = slice(start, start + chunk)
        rows = jnp.concatenate([even_ref[:, cols], odd_ref[:, cols]], axis=0)
        gate_pre += jnp.dot(rows, gate_ref[cols, :], preferred_element_type=f32)
        up_pre += jnp.dot(rows, up_ref[cols, :], preferred_element_type=f32)
        hidden_grad += lax.dot_general(rows, down_ref[:, cols], NT, preferred_element_type=f32)
    is_token = lax.broadcasted_iota(jnp.int32, (count, units), 0) % PAIR < CAP
    hidden_grad = pltpu.roll(hidden_grad, count - CAP, 0)
    sigmoid_gate = jax.nn.sigmoid(gate_pre)
    silu_gate = gate_pre * sigmoid_gate
    hidden = silu_gate * up_pre
    silu_slope = sigmoid_gate * (1.0 + gate_pre * (1.0 - sigmoid_gate))
    gate_grad = pltpu.roll(hidden_grad * up_pre * silu_slope, CAP, 0)
    up_grad = pltpu.roll(hidden_grad * silu_gate, CAP, 0)
    hidden = jnp.where(is_token, hidden, 0.0).astype(bf16)
    gate_grad = jnp.where(is_token, 0.0, gate_grad).astype(bf16)
    up_grad = jnp.where(is_token, 0.0, up_grad).astype(bf16)
    for start in range(0, width, chunk):
        cols = slice(start, start + chunk)
        part = jnp.dot(hidden, down_ref[:, cols], preferred_element_type=f32)
        part += lax.dot_general(gate_grad, gate_ref[cols, :], NT, preferred_element_type=f32)
        part += lax.dot_general(up_grad, up_ref[cols, :], NT, preferred_element_type=f32)
        part = part.astype(bf16)
        even_out[:, cols] = part[:half]
        odd_out[:, cols] = part[half:]


def expert_rows(even, odd, w_gate, w_up, w_down):
    half, width = even.shape
    units = w_down.shape[0]
    vmem = pl.BlockSpec(memory_space=pltpu.VMEM)
    return pl.pallas_call(
        functools.partial(expert_kernel, chunk_of(width, 1024)),
        in_specs=[vmem] * 5,
        out_specs=[vmem] * 2,
        out_shape=[jax.ShapeDtypeStruct((half, width), bf16)] * 2,
        compiler_params=pltpu.CompilerParams(vmem_limit_bytes=40 * MIB),
        cost_estimate=pl.CostEstimate(
            flops=24 * half * width * units,
            bytes_accessed=6 * width * units + 8 * half * width,
            transcendentals=2 * half * units,
        ),
        name="expert_rows",
    )(even, odd, w_gate, w_up, w_down)


def thirds(x):
    high = x.astype(bf16)
    rest = x - high.astype(f32)
    middle = rest.astype(bf16)
    return high, middle, (rest - middle.astype(f32)).astype(bf16)


def finish_kernel(
    experts, n_terms, routes_ref, probs_ref, tokens_ref, grads_ref, *refs
):
    term_refs = refs[:n_terms]
    layer_ref, input_ref, prob_grad_ref, place_ref, weight_ref, dot_ref = refs[n_terms:]
    count = tokens_ref.shape[0]
    step = pl.program_id(0)

    @pl.when(step == 0)
    def _():
        for e in range(experts):
            matches, place = slot_places(routes_ref[...], e)
            place_ref[e] = place
            weight_ref[e] = slot_probs(matches, place, probs_ref[...])
            dot_ref[e] = jnp.zeros((PAIR, 1), f32)

    tokens = tokens_ref[...].astype(f32)
    grads = grads_ref[...].astype(f32)
    for e in range(experts):
        place = place_ref[e]
        total = term_refs[0][e].astype(f32)
        for ref in term_refs[1:]:
            total += ref[e].astype(f32)
        is_token = lax.broadcasted_iota(jnp.int32, total.shape, 0) < CAP
        mixed = jnp.where(is_token, weight_ref[e] * total, total)
        high, middle, low = thirds(mixed)
        values = jnp.concatenate([high.astype(f32), middle.astype(f32), low.astype(f32)], axis=0).astype(bf16)
        token_row = lax.broadcasted_iota(jnp.int32, place.shape, 0) < CAP
        to_layer = jnp.where(token_row, place, 0.0)
        to_input = jnp.where(token_row, 0.0, place)
        adder = jnp.concatenate([to_layer, to_input], axis=1)
        adder = jnp.concatenate([adder, adder, adder], axis=0).astype(bf16)
        added = lax.dot_general(adder, values, TN, preferred_element_type=f32)
        tokens += added[:count]
        grads += added[count:]
        grad_rows = jnp.dot(place.astype(bf16), grads_ref[...], preferred_element_type=f32)
        dot_ref[e] += jnp.sum(grad_rows * total, axis=1, keepdims=True)
    layer_ref[...] = tokens.astype(bf16)
    input_ref[...] = grads.astype(bf16)

    @pl.when(step == pl.num_programs(0) - 1)
    def _():
        result = jnp.zeros(routes_ref.shape, f32)
        for e in range(experts):
            token_row = lax.broadcasted_iota(jnp.int32, (PAIR, count), 0) < CAP
            token_dot = jnp.sum(jnp.where(token_row, place_ref[e] * dot_ref[e], 0.0), axis=0, keepdims=True)
            result += jnp.where(routes_ref[...] == e, token_dot, 0.0)
        prob_grad_ref[...] = result


def finish(routes, probs, tokens, grads, terms, experts):
    count, width = tokens.shape
    chunk = chunk_of(width, 1792)
    topk = routes.shape[0]
    whole = lambda i: (0, 0)
    across = pl.BlockSpec((count, chunk), lambda i: (0, i))
    return pl.pallas_call(
        functools.partial(finish_kernel, experts, len(terms)),
        grid=(width // chunk,),
        in_specs=[pl.BlockSpec((topk, count), whole), pl.BlockSpec((topk, count), whole), across, across]
        + [pl.BlockSpec((experts, PAIR, chunk), lambda i: (0, 0, i))] * len(terms),
        out_specs=[across, across, pl.BlockSpec((topk, count), whole)],
        out_shape=[
            jax.ShapeDtypeStruct((count, width), bf16),
            jax.ShapeDtypeStruct((count, width), bf16),
            jax.ShapeDtypeStruct((topk, count), f32),
        ],
        scratch_shapes=[
            pltpu.VMEM((experts, PAIR, count), f32),
            pltpu.VMEM((experts, PAIR, 1), f32),
            pltpu.VMEM((experts, PAIR, 1), f32),
        ],
        compiler_params=pltpu.CompilerParams(vmem_limit_bytes=32 * MIB),
        cost_estimate=pl.CostEstimate(
            flops=16 * experts * PAIR * count * width, bytes_accessed=8 * count * width, transcendentals=0
        ),
        name="finish",
    )(routes, probs, tokens, grads, *terms)


def local(tokens, out_grad, routes, gate_probs, w_gate, w_up, w_down):
    experts = lax.axis_size(AXIS) // PANELS
    width = tokens.shape[1]
    rows = PAIR * experts
    peers = [[e * PANELS + r for e in range(experts)] for r in range(PANELS)]
    send = pick(routes.T, gate_probs.T, tokens, out_grad, experts)
    if experts > 1:
        send = lax.all_to_all(send, AXIS, 0, 0, axis_index_groups=peers, tiled=True)
    even, odd = gather_rows(send.reshape(rows, width))
    even, odd = expert_rows(even, odd, w_gate, w_up, w_down)
    terms = scatter_sum(even, odd)
    if experts > 1:
        terms = [functools.reduce(jnp.add, [t.astype(f32) for t in terms])]
    terms = [t.reshape(experts, PAIR, width) for t in terms]
    if experts > 1:
        terms = [lax.all_to_all(terms[0], AXIS, 0, 0, axis_index_groups=peers, tiled=True)]
    layer_out, input_grad, prob_grad = finish(routes.T, gate_probs.T, tokens, out_grad, terms, experts)
    return layer_out, input_grad, prob_grad.T


def solution(mesh):
    rows = P(("groups", AXIS), None)
    return jax.shard_map(
        local,
        mesh=mesh,
        in_specs=(rows, rows, rows, rows, P(None, AXIS), P(None, AXIS), P(AXIS, None)),
        out_specs=(rows, rows, rows),
        check_vma=False,
    )
```

time: 94.9 us -> 65.9 us (0.69)
  matrix products: 17.5 us -> 0 us
  local copies, waits for them, and re-layouts: 19.2 us -> 4.51 us
  other arithmetic: 9.65 us -> 0.34 us
  Pallas kernels: 0 us -> 9.11 us
  waiting for transfers between devices: 27.1 us -> 30.8 us
    dot_general x10 -> x0, matrix products: 17.5 us -> none  [the longest x1 4.45 us: local(): jnp.dot(mixing, out_sum, precision=highest, preferred_element_type=f32)]
    pallas_call x0 -> x3, Pallas kernels: none -> 9.11 us  [the longest x1 4.13 us: finish(): pl.pallas_call(functools.partial(finish_kernel, experts, len(terms)), gri...]
    another operation x5 -> x1, other arithmetic: 7.48 us -> 0.23 us  [the longest x1 3.87 us: local(): jnp.stack([out_rows.reshape(-1, CAP, width), input_rows.reshape(-1, CAP,...]
    another operation x6 -> x0, local copies, waits for them, and re-layouts: 6.77 us -> none  [the longest x2 3.86 us: local(): jnp.stack([out_rows.reshape(-1, CAP, width), input_rows.reshape(-1, CAP,...]
    reshape x1 -> x0, local copies, waits for them, and re-layouts: 4.04 us -> none  [local(): everyone = jnp.stack([even, odd]).reshape(-1, 2, CAP, width)]
    ppermute x16, waiting for transfers between devices: 27.1 us -> 30.8 us  [swap(): return lax.ppermute(x, AXIS, [(i, i ^ offset) for i in range(devices)])]
    unnamed x22 -> x29, local copies, waits for them, and re-layouts: 0.8 us -> 4.47 us
    slice x1, local copies, waits for them, and re-layouts: 3.01 us -> 0.03 us  [scatter_sum(): part[2 * far + 1].astype(bf16)]
  transfers between devices with their start and end apart: 16 -> 16, of which waited for: 9 -> 11; matrix products, arithmetic and copies ran while one was open for 3% -> 0% of each run, Pallas kernels for 0% -> 0%
where the time goes in v2:
time: 65.9 us; the launch traced here: 65.6 us
  waiting for transfers between devices  30.8 us (47%)
  starting transfers between devices  20 us (30%)
  Pallas kernels  9.11 us (14%)
  local copies, waits for them, and re-layouts  4.51 us (7%)
  between operations  0.82 us (1%)
    ppermute x16, waiting for transfers between devices, swap(): return lax.ppermute(x, AXIS, [(i, i ^ offset) for i in range(devices)])  30.8 us
    ppermute x16, starting transfers between devices, swap(): return lax.ppermute(x, AXIS, [(i, i ^ offset) for i in range(devices)])  20 us
    unnamed x29, local copies, waits for them, and re-layouts  4.47 us
    pallas_call x1, Pallas kernels, finish(): pl.pallas_call(functools.partial(finish_kernel, experts, len(terms)), gri...  4.13 us
    pallas_call x1, Pallas kernels, expert_rows(): pl.pallas_call(functools.partial(expert_kernel, chunk_of(width, 1024)), i...  3.56 us
    pallas_call x1, Pallas kernels, pick(): pl.pallas_call(functools.partial(pick_kernel, experts), grid=(width // ch...  1.42 us
  transfers between devices with their start and end apart: 16, of which 11 were waited for; matrix products, arithmetic and copies ran while one was open for 0% of the time, Pallas kernels for 0%

profile of v2, /device:TPU:0, one launch (start us, length us, event | category | flops | bytes accessed | tf_op | source)
XLA Modules:
  0.0 65.6 jit_solution(15346733164749359708)
XLA Ops:
  0.6 1.5 %copy-done = bf16[128,7168]{1,0:T(8,128)(2,1)S(1)} copy-done((bf16[128,7168]{1,0:T(8,128)(2,1)S(1)}, bf16[128,7168]{1,0:T(8,128)(2,1)}, u32[]{:S(2)}) %copy-start) | copy-done | bytes 1835032
  2.1 1.5 %copy-done.2 = bf16[128,7168]{1,0:T(8,128)(2,1)S(1)} copy-done((bf16[128,7168]{1,0:T(8,128)(2,1)S(1)}, bf16[128,7168]{1,0:T(8,128)(2,1)}, u32[]{:S(2)}) %copy-start.2) | copy-done | bytes 1835032
  3.6 0.7 %copy-done.7 = s32[128,8]{0,1:T(8,128)S(1)} copy-done((s32[128,8]{0,1:T(8,128)S(1)}, s32[128,8]{0,1:T(8,128)}, u32[]{:S(2)}) %copy-start.7) | copy-done | bytes 4120
  4.3 0.7 %copy-done.9 = f32[128,8]{0,1:T(8,128)S(1)} copy-done((f32[128,8]{0,1:T(8,128)S(1)}, f32[128,8]{0,1:T(8,128)}, u32[]{:S(2)}) %copy-start.9) | copy-done | bytes 4120
  5.0 1.4 %pick_rows.1 = bf16[1,8,7168]{2,1,0:T(8,128)(2,1)S(1)} custom-call(s32[8,128]{1,0:T(8,128)S(1)} %bitcast.17, f32[8,128]{1,0:T(8,128)S(1)} %bitcast.19, bf16[128,7168]{1,0:T(8,128)(2,1)S(1)} %copy-done, bf16[128,7168]{1,0:T(8,128)(2,1)S(1)} %copy-done.2), custom_call_target="tpu_custom_call" | custom-call | flops 29360128 | bytes 3670016 | tf_op jit(solution)/shard_map/pick_rows/pallas_call | solution.py:95
  6.5 5.1 %collective-permute-start.5 = (bf16[8,7168]{1,0:T(8,128)(2,1)S(1)}, bf16[8,7168]{1,0:T(8,128)(2,1)S(1)}, u32[]{:S(2)}, u32[]{:S(2)}) collective-permute-start(bf16[8,7168]{1,0:T(8,128)(2,1)S(1)} %bitcast.10), channel_id=1, source_target_pairs={{0,12},{1,13},{2,14},{3,15},{4,8},{5,9},{6,10},{7,11},{8,4},{9,5},... | collective-permute-start | bytes 344072 | tf_op jit(solution)/shard_map/ppermute | solution.py:30
  11.6 0.6 collective-permute-start.1
  12.2 1.7 %collective-permute-start = (bf16[8,7168]{1,0:T(8,128)(2,1)S(1)}, bf16[8,7168]{1,0:T(8,128)(2,1)S(1)}, u32[]{:S(2)}, u32[]{:S(2)}) collective-permute-start(bf16[8,7168]{1,0:T(8,128)(2,1)S(1)} %bitcast.13), channel_id=1, source_target_pairs={{0,2},{1,3},{2,0},{3,1},{4,6},{5,7},{6,4},{7,5},{8,10},{9,11},{10,... | collective-permute-start | bytes 344072 | tf_op jit(solution)/shard_map/ppermute | solution.py:30
  13.9 1.8 %collective-permute-done.5 = bf16[8,7168]{1,0:T(8,128)(2,1)S(1)} collective-permute-done((bf16[8,7168]{1,0:T(8,128)(2,1)S(1)}, bf16[8,7168]{1,0:T(8,128)(2,1)S(1)}, u32[]{:S(2)}, u32[]{:S(2)}) %collective-permute-start.5) | collective-permute-done | bytes 114720 | tf_op jit(solution)/shard_map/ppermute | solution.py:30
  15.6 1.7 %collective-permute-start.6 = (bf16[8,7168]{1,0:T(8,128)(2,1)S(1)}, bf16[8,7168]{1,0:T(8,128)(2,1)S(1)}, u32[]{:S(2)}, u32[]{:S(2)}) collective-permute-start(bf16[8,7168]{1,0:T(8,128)(2,1)S(1)} %collective-permute-done.5), channel_id=1, source_target_pairs={{0,2},{1,3},{2,0},{3,1},{4,6},{5,7},{6,4},{7,5},{8,10},{9,11},{10,... | collective-permute-start | bytes 344072 | tf_op jit(solution)/shard_map/ppermute | solution.py:30
  17.4 3.9 %collective-permute-done.3 = bf16[8,7168]{1,0:T(8,128)(2,1)S(1)} collective-permute-done((bf16[8,7168]{1,0:T(8,128)(2,1)S(1)}, bf16[8,7168]{1,0:T(8,128)(2,1)S(1)}, u32[]{:S(2)}, u32[]{:S(2)}) %collective-permute-start.3) | collective-permute-done | bytes 114720 | tf_op jit(solution)/shard_map/ppermute | solution.py:30
  21.2 1.5 %collective-permute-start.4 = (bf16[8,7168]{1,0:T(8,128)(2,1)S(1)}, bf16[8,7168]{1,0:T(8,128)(2,1)S(1)}, u32[]{:S(2)}, u32[]{:S(2)}) collective-permute-start(bf16[8,7168]{1,0:T(8,128)(2,1)S(1)} %collective-permute-done.3), channel_id=1, source_target_pairs={{0,2},{1,3},{2,0},{3,1},{4,6},{5,7},{6,4},{7,5},{8,10},{9,11},{10,... | collective-permute-start | bytes 344072 | tf_op jit(solution)/shard_map/ppermute | solution.py:30
  22.8 0.5 collective-permute-start.2
  23.3 4.6 %collective-permute-done.2 = bf16[8,7168]{1,0:T(8,128)(2,1)S(1)} collective-permute-done((bf16[8,7168]{1,0:T(8,128)(2,1)S(1)}, bf16[8,7168]{1,0:T(8,128)(2,1)S(1)}, u32[]{:S(2)}, u32[]{:S(2)}) %collective-permute-start.2) | collective-permute-done | bytes 114720 | tf_op jit(solution)/shard_map/ppermute | solution.py:30
  28.1 2.5 %collective-permute-done.7.odd_ref = bf16[64,7168]{1,0:T(8,128)(2,1)S(1)} collective-permute-done((bf16[64,7168]{1,0:T(8,128)(2,1)S(1)}, bf16[64,7168]{1,0:T(8,128)(2,1)S(1)}, u32[]{:S(2)}, u32[]{:S(2)}) %collective-permute-start.7) | collective-permute-done | bytes 917536 | tf_op jit(solution)/shard_map/ppermute | solution.py:30
  30.6 3.6 %expert_rows.1 = (bf16[64,7168]{1,0:T(8,128)(2,1)S(1)}, bf16[64,7168]{1,0:T(8,128)(2,1)S(1)}) custom-call(bf16[64,7168]{1,0:T(8,128)(2,1)S(1)} %constant_dynamic-update-slice_fusion.even_ref, bf16[64,7168]{1,0:T(8,128)(2,1)S(1)} %collective-permute-done.7.odd_ref, bf16[7168,128]{1,0:T(8,128)(2,1)S(1)} %copy-done.4, bf16[7168,128]{1,0:T(8,128)(2,1)S(1)} %copy-done.5, ...), custom_call_target="tpu_custom_call" | custom-call | flops 1409286144 | bytes 9175040 | tf_op jit(solution)/shard_map/expert_rows/pallas_call | solution.py:153
  34.3 2.3 %collective-permute-done.8 = bf16[64,7168]{1,0:T(8,128)(2,1)S(1)} collective-permute-done((bf16[64,7168]{1,0:T(8,128)(2,1)S(1)}, bf16[64,7168]{1,0:T(8,128)(2,1)S(1)}, u32[]{:S(2)}, u32[]{:S(2)}) %collective-permute-start.8) | collective-permute-done | bytes 917536 | tf_op jit(solution)/shard_map/ppermute | solution.py:30
  36.7 0.2 fusion.4
  37.0 1.6 %collective-permute-start.14 = (bf16[8,7168]{1,0:T(8,128)(2,1)S(1)}, bf16[8,7168]{1,0:T(8,128)(2,1)S(1)}, u32[]{:S(2)}, u32[]{:S(2)}) collective-permute-start(bf16[8,7168]{1,0:T(8,128)(2,1)S(1)} %get-tuple-element.19), channel_id=1, source_target_pairs={{0,2},{1,3},{2,0},{3,1},{4,6},{5,7},{6,4},{7,5},{8,10},{9,11},{10,... | collective-permute-start | bytes 344072 | tf_op jit(solution)/shard_map/ppermute | solution.py:30
  38.6 0.5 collective-permute-start.12
  39.1 1.5 %collective-permute-start.10 = (bf16[8,7168]{1,0:T(8,128)(2,1)S(1)}, bf16[8,7168]{1,0:T(8,128)(2,1)S(1)}, u32[]{:S(2)}, u32[]{:S(2)}) collective-permute-start(bf16[8,7168]{1,0:T(8,128)(2,1)S(1)} %get-tuple-element.21), channel_id=1, source_target_pairs={{0,2},{1,3},{2,0},{3,1},{4,6},{5,7},{6,4},{7,5},{8,10},{9,11},{10,... | collective-permute-start | bytes 344072 | tf_op jit(solution)/shard_map/ppermute | solution.py:30
  40.6 0.5 collective-permute-start.9
  41.1 1.9 %collective-permute-done.14 = bf16[8,7168]{1,0:T(8,128)(2,1)S(1)} collective-permute-done((bf16[8,7168]{1,0:T(8,128)(2,1)S(1)}, bf16[8,7168]{1,0:T(8,128)(2,1)S(1)}, u32[]{:S(2)}, u32[]{:S(2)}) %collective-permute-start.14) | collective-permute-done | bytes 114720 | tf_op jit(solution)/shard_map/ppermute | solution.py:30
  43.1 2.5 %collective-permute-done.12 = bf16[8,7168]{1,0:T(8,128)(2,1)S(1)} collective-permute-done((bf16[8,7168]{1,0:T(8,128)(2,1)S(1)}, bf16[8,7168]{1,0:T(8,128)(2,1)S(1)}, u32[]{:S(2)}, u32[]{:S(2)}) %collective-permute-start.12) | collective-permute-done | bytes 114720 | tf_op jit(solution)/shard_map/ppermute | solution.py:30
  45.5 2.5 %collective-permute-done.10 = bf16[8,7168]{1,0:T(8,128)(2,1)S(1)} collective-permute-done((bf16[8,7168]{1,0:T(8,128)(2,1)S(1)}, bf16[8,7168]{1,0:T(8,128)(2,1)S(1)}, u32[]{:S(2)}, u32[]{:S(2)}) %collective-permute-start.10) | collective-permute-done | bytes 114720 | tf_op jit(solution)/shard_map/ppermute | solution.py:30
  48.0 1.7 %collective-permute-done.9 = bf16[8,7168]{1,0:T(8,128)(2,1)S(1)} collective-permute-done((bf16[8,7168]{1,0:T(8,128)(2,1)S(1)}, bf16[8,7168]{1,0:T(8,128)(2,1)S(1)}, u32[]{:S(2)}, u32[]{:S(2)}) %collective-permute-start.9) | collective-permute-done | bytes 114720 | tf_op jit(solution)/shard_map/ppermute | solution.py:30
  49.7 0.6 collective-permute-start.15
  50.4 2.3 %collective-permute-start.13 = (bf16[8,7168]{1,0:T(8,128)(2,1)S(1)}, bf16[8,7168]{1,0:T(8,128)(2,1)S(1)}, u32[]{:S(2)}, u32[]{:S(2)}) collective-permute-start(bf16[8,7168]{1,0:T(8,128)(2,1)S(1)} %get-tuple-element.14), channel_id=1, source_target_pairs={{0,8},{1,9},{2,10},{3,11},{4,12},{5,13},{6,14},{7,15},{8,0},{9,1},... | collective-permute-start | bytes 344072 | tf_op jit(solution)/shard_map/ppermute | solution.py:30
  52.7 1.5 %collective-permute-start.11 = (bf16[8,7168]{1,0:T(8,128)(2,1)S(1)}, bf16[8,7168]{1,0:T(8,128)(2,1)S(1)}, u32[]{:S(2)}, u32[]{:S(2)}) collective-permute-start(bf16[8,7168]{1,0:T(8,128)(2,1)S(1)} %get-tuple-element.15), channel_id=1, source_target_pairs={{0,12},{1,13},{2,14},{3,15},{4,8},{5,9},{6,10},{7,11},{8,4},{9,5},... | collective-permute-start | bytes 344072 | tf_op jit(solution)/shard_map/ppermute | solution.py:30
  54.2 1.3 %collective-permute-done.15 = bf16[8,7168]{1,0:T(8,128)(2,1)S(1)} collective-permute-done((bf16[8,7168]{1,0:T(8,128)(2,1)S(1)}, bf16[8,7168]{1,0:T(8,128)(2,1)S(1)}, u32[]{:S(2)}, u32[]{:S(2)}) %collective-permute-start.15) | collective-permute-done | bytes 114720 | tf_op jit(solution)/shard_map/ppermute | solution.py:30
  55.5 6.0 %collective-permute-done.13 = bf16[8,7168]{1,0:T(8,128)(2,1)S(1)} collective-permute-done((bf16[8,7168]{1,0:T(8,128)(2,1)S(1)}, bf16[8,7168]{1,0:T(8,128)(2,1)S(1)}, u32[]{:S(2)}, u32[]{:S(2)}) %collective-permute-start.13) | collective-permute-done | bytes 114720 | tf_op jit(solution)/shard_map/ppermute | solution.py:30
  61.5 4.1 %finish.1 = (bf16[128,7168]{1,0:T(8,128)(2,1)}, bf16[128,7168]{1,0:T(8,128)(2,1)}, f32[8,128]{1,0:T(8,128)}) custom-call(s32[8,128]{1,0:T(8,128)S(1)} %bitcast.18, f32[8,128]{1,0:T(8,128)S(1)} %bitcast.20, bf16[128,7168]{1,0:T(8,128)(2,1)S(1)} %copy-done.1, bf16[128,7168]{1,0:T(8,128)(2,1)S(1)} %copy-done.3, f32[1,8,7168]{2,1,0:T(8,128)S(1)} %get-tuple-element.16.refs_0_, ...), custom_call_target="tpu_custom_call" | custom-call | flops 117440512 | bytes 7340032 | tf_op jit(solution)/shard_map/finish/pallas_call | solution.py:231
  (36 shorter events, 0.5 us)
Async XLA Ops:
  0.6 1.5 %copy-start = (bf16[128,7168]{1,0:T(8,128)(2,1)S(1)}, bf16[128,7168]{1,0:T(8,128)(2,1)}, u32[]{:S(2)}) copy-start(bf16[128,7168]{1,0:T(8,128)(2,1)} %tokens_ref.3) | copy-start | bytes 5505028
  2.1 1.5 %copy-start.2 = (bf16[128,7168]{1,0:T(8,128)(2,1)S(1)}, bf16[128,7168]{1,0:T(8,128)(2,1)}, u32[]{:S(2)}) copy-start(bf16[128,7168]{1,0:T(8,128)(2,1)} %grads_ref.3) | copy-start | bytes 5505028
  3.6 0.7 %copy-start.7 = (s32[128,8]{0,1:T(8,128)S(1)}, s32[128,8]{0,1:T(8,128)}, u32[]{:S(2)}) copy-start(s32[128,8]{0,1:T(8,128)} %param.9) | copy-start | bytes 12292
  4.3 0.7 %copy-start.9 = (f32[128,8]{0,1:T(8,128)S(1)}, f32[128,8]{0,1:T(8,128)}, u32[]{:S(2)}) copy-start(f32[128,8]{0,1:T(8,128)} %param.10) | copy-start | bytes 12292
  5.0 25.6 %copy-start.5 = (bf16[7168,128]{1,0:T(8,128)(2,1)S(1)}, bf16[7168,128]{1,0:T(8,128)(2,1)}, u32[]{:S(2)}) copy-start(bf16[7168,128]{1,0:T(8,128)(2,1)} %up_ref.1) | copy-start | bytes 5505028
  5.0 25.6 %copy-start.6 = (bf16[128,7168]{1,0:T(8,128)(2,1)S(1)}, bf16[128,7168]{1,0:T(8,128)(2,1)}, u32[]{:S(2)}) copy-start(bf16[128,7168]{1,0:T(8,128)(2,1)} %down_ref.1) | copy-start | bytes 5505028
  6.4 24.1 %copy-start.4 = (bf16[7168,128]{1,0:T(8,128)(2,1)S(1)}, bf16[7168,128]{1,0:T(8,128)(2,1)}, u32[]{:S(2)}) copy-start(bf16[7168,128]{1,0:T(8,128)(2,1)} %gate_ref.1) | copy-start | bytes 5505028
  6.5 9.2 %collective-permute-start.5 = (bf16[8,7168]{1,0:T(8,128)(2,1)S(1)}, bf16[8,7168]{1,0:T(8,128)(2,1)S(1)}, u32[]{:S(2)}, u32[]{:S(2)}) collective-permute-start(bf16[8,7168]{1,0:T(8,128)(2,1)S(1)} %bitcast.10), channel_id=1, source_target_pairs={{0,12},{1,13},{2,14},{3,15},{4,8},{5,9},{6,10},{7,11},{8,4},{9,5},... | collective-permute-start | bytes 344072 | tf_op jit(solution)/shard_map/ppermute | solution.py:30
  11.6 9.7 %collective-permute-start.3 = (bf16[8,7168]{1,0:T(8,128)(2,1)S(1)}, bf16[8,7168]{1,0:T(8,128)(2,1)S(1)}, u32[]{:S(2)}, u32[]{:S(2)}) collective-permute-start(bf16[8,7168]{1,0:T(8,128)(2,1)S(1)} %bitcast.11), channel_id=1, source_target_pairs={{0,8},{1,9},{2,10},{3,11},{4,12},{5,13},{6,14},{7,15},{8,0},{9,1},... | collective-permute-start | bytes 344072 | tf_op jit(solution)/shard_map/ppermute | solution.py:30
  11.6 11.2 %collective-permute-start.1 = (bf16[8,7168]{1,0:T(8,128)(2,1)S(1)}, bf16[8,7168]{1,0:T(8,128)(2,1)S(1)}, u32[]{:S(2)}, u32[]{:S(2)}) collective-permute-start(bf16[8,7168]{1,0:T(8,128)(2,1)S(1)} %bitcast.12), channel_id=1, source_target_pairs={{0,4},{1,5},{2,6},{3,7},{4,0},{5,1},{6,2},{7,3},{8,12},{9,13},{10,... | collective-permute-start | bytes 344072 | tf_op jit(solution)/shard_map/ppermute | solution.py:30
  12.2 11.1 %collective-permute-start = (bf16[8,7168]{1,0:T(8,128)(2,1)S(1)}, bf16[8,7168]{1,0:T(8,128)(2,1)S(1)}, u32[]{:S(2)}, u32[]{:S(2)}) collective-permute-start(bf16[8,7168]{1,0:T(8,128)(2,1)S(1)} %bitcast.13), channel_id=1, source_target_pairs={{0,2},{1,3},{2,0},{3,1},{4,6},{5,7},{6,4},{7,5},{8,10},{9,11},{10,... | collective-permute-start | bytes 344072 | tf_op jit(solution)/shard_map/ppermute | solution.py:30
  15.6 12.3 %collective-permute-start.6 = (bf16[8,7168]{1,0:T(8,128)(2,1)S(1)}, bf16[8,7168]{1,0:T(8,128)(2,1)S(1)}, u32[]{:S(2)}, u32[]{:S(2)}) collective-permute-start(bf16[8,7168]{1,0:T(8,128)(2,1)S(1)} %collective-permute-done.5), channel_id=1, source_target_pairs={{0,2},{1,3},{2,0},{3,1},{4,6},{5,7},{6,4},{7,5},{8,10},{9,11},{10,... | collective-permute-start | bytes 344072 | tf_op jit(solution)/shard_map/ppermute | solution.py:30
  21.2 6.7 %collective-permute-start.4 = (bf16[8,7168]{1,0:T(8,128)(2,1)S(1)}, bf16[8,7168]{1,0:T(8,128)(2,1)S(1)}, u32[]{:S(2)}, u32[]{:S(2)}) collective-permute-start(bf16[8,7168]{1,0:T(8,128)(2,1)S(1)} %collective-permute-done.3), channel_id=1, source_target_pairs={{0,2},{1,3},{2,0},{3,1},{4,6},{5,7},{6,4},{7,5},{8,10},{9,11},{10,... | collective-permute-start | bytes 344072 | tf_op jit(solution)/shard_map/ppermute | solution.py:30
  22.8 5.2 %collective-permute-start.2 = (bf16[8,7168]{1,0:T(8,128)(2,1)S(1)}, bf16[8,7168]{1,0:T(8,128)(2,1)S(1)}, u32[]{:S(2)}, u32[]{:S(2)}) collective-permute-start(bf16[8,7168]{1,0:T(8,128)(2,1)S(1)} %collective-permute-done.1), channel_id=1, source_target_pairs={{0,2},{1,3},{2,0},{3,1},{4,6},{5,7},{6,4},{7,5},{8,10},{9,11},{10,... | collective-permute-start | bytes 344072 | tf_op jit(solution)/shard_map/ppermute | solution.py:30
  28.0 2.5 %collective-permute-start.7 = (bf16[64,7168]{1,0:T(8,128)(2,1)S(1)}, bf16[64,7168]{1,0:T(8,128)(2,1)S(1)}, u32[]{:S(2)}, u32[]{:S(2)}) collective-permute-start(bf16[64,7168]{1,0:T(8,128)(2,1)S(1)} %constant_dynamic-update-slice_fusion.even_ref), channel_id=1, source_target_pairs={{0,1},{1,0},{2,3},{3,2},{4,5},{5,4},{6,7},{7,6},{8,9},{9,8},{10,11... | collective-permute-start | bytes 2752520 | tf_op jit(solution)/shard_map/ppermute | solution.py:30
  34.1 2.5 %collective-permute-start.8 = (bf16[64,7168]{1,0:T(8,128)(2,1)S(1)}, bf16[64,7168]{1,0:T(8,128)(2,1)S(1)}, u32[]{:S(2)}, u32[]{:S(2)}) collective-permute-start(bf16[64,7168]{1,0:T(8,128)(2,1)S(1)} %get-tuple-element.9), channel_id=1, source_target_pairs={{0,1},{1,0},{2,3},{3,2},{4,5},{5,4},{6,7},{7,6},{8,9},{9,8},{10,11... | collective-permute-start | bytes 2752520 | tf_op jit(solution)/shard_map/ppermute | solution.py:30
  36.7 24.8 %copy-start.3 = (bf16[128,7168]{1,0:T(8,128)(2,1)S(1)}, bf16[128,7168]{1,0:T(8,128)(2,1)}, u32[]{:S(2)}) copy-start(bf16[128,7168]{1,0:T(8,128)(2,1)} %grads_ref.3) | copy-start | bytes 5505028
  36.9 24.6 %copy-start.1 = (bf16[128,7168]{1,0:T(8,128)(2,1)S(1)}, bf16[128,7168]{1,0:T(8,128)(2,1)}, u32[]{:S(2)}) copy-start(bf16[128,7168]{1,0:T(8,128)(2,1)} %tokens_ref.3) | copy-start | bytes 5505028
  36.9 24.6 %copy-start.8 = (s32[128,8]{0,1:T(8,128)S(1)}, s32[128,8]{0,1:T(8,128)}, u32[]{:S(2)}) copy-start(s32[128,8]{0,1:T(8,128)} %param.9) | copy-start | bytes 12292
  36.9 24.6 %copy-start.10 = (f32[128,8]{0,1:T(8,128)S(1)}, f32[128,8]{0,1:T(8,128)}, u32[]{:S(2)}) copy-start(f32[128,8]{0,1:T(8,128)} %param.10) | copy-start | bytes 12292
  37.0 6.1 %collective-permute-start.14 = (bf16[8,7168]{1,0:T(8,128)(2,1)S(1)}, bf16[8,7168]{1,0:T(8,128)(2,1)S(1)}, u32[]{:S(2)}, u32[]{:S(2)}) collective-permute-start(bf16[8,7168]{1,0:T(8,128)(2,1)S(1)} %get-tuple-element.19), channel_id=1, source_target_pairs={{0,2},{1,3},{2,0},{3,1},{4,6},{5,7},{6,4},{7,5},{8,10},{9,11},{10,... | collective-permute-start | bytes 344072 | tf_op jit(solution)/shard_map/ppermute | solution.py:30
  38.6 6.9 %collective-permute-start.12 = (bf16[8,7168]{1,0:T(8,128)(2,1)S(1)}, bf16[8,7168]{1,0:T(8,128)(2,1)S(1)}, u32[]{:S(2)}, u32[]{:S(2)}) collective-permute-start(bf16[8,7168]{1,0:T(8,128)(2,1)S(1)} %get-tuple-element.20), channel_id=1, source_target_pairs={{0,2},{1,3},{2,0},{3,1},{4,6},{5,7},{6,4},{7,5},{8,10},{9,11},{10,... | collective-permute-start | bytes 344072 | tf_op jit(solution)/shard_map/ppermute | solution.py:30
  39.1 8.9 %collective-permute-start.10 = (bf16[8,7168]{1,0:T(8,128)(2,1)S(1)}, bf16[8,7168]{1,0:T(8,128)(2,1)S(1)}, u32[]{:S(2)}, u32[]{:S(2)}) collective-permute-start(bf16[8,7168]{1,0:T(8,128)(2,1)S(1)} %get-tuple-element.21), channel_id=1, source_target_pairs={{0,2},{1,3},{2,0},{3,1},{4,6},{5,7},{6,4},{7,5},{8,10},{9,11},{10,... | collective-permute-start | bytes 344072 | tf_op jit(solution)/shard_map/ppermute | solution.py:30
  40.6 9.0 %collective-permute-start.9 = (bf16[8,7168]{1,0:T(8,128)(2,1)S(1)}, bf16[8,7168]{1,0:T(8,128)(2,1)S(1)}, u32[]{:S(2)}, u32[]{:S(2)}) collective-permute-start(bf16[8,7168]{1,0:T(8,128)(2,1)S(1)} %get-tuple-element.22), channel_id=1, source_target_pairs={{0,2},{1,3},{2,0},{3,1},{4,6},{5,7},{6,4},{7,5},{8,10},{9,11},{10,... | collective-permute-start | bytes 344072 | tf_op jit(solution)/shard_map/ppermute | solution.py:30
  49.7 5.8 %collective-permute-start.15 = (bf16[8,7168]{1,0:T(8,128)(2,1)S(1)}, bf16[8,7168]{1,0:T(8,128)(2,1)S(1)}, u32[]{:S(2)}, u32[]{:S(2)}) collective-permute-start(bf16[8,7168]{1,0:T(8,128)(2,1)S(1)} %get-tuple-element.13), channel_id=1, source_target_pairs={{0,4},{1,5},{2,6},{3,7},{4,0},{5,1},{6,2},{7,3},{8,12},{9,13},{10,... | collective-permute-start | bytes 344072 | tf_op jit(solution)/shard_map/ppermute | solution.py:30
  50.4 11.1 %collective-permute-start.13 = (bf16[8,7168]{1,0:T(8,128)(2,1)S(1)}, bf16[8,7168]{1,0:T(8,128)(2,1)S(1)}, u32[]{:S(2)}, u32[]{:S(2)}) collective-permute-start(bf16[8,7168]{1,0:T(8,128)(2,1)S(1)} %get-tuple-element.14), channel_id=1, source_target_pairs={{0,8},{1,9},{2,10},{3,11},{4,12},{5,13},{6,14},{7,15},{8,0},{9,1},... | collective-permute-start | bytes 344072 | tf_op jit(solution)/shard_map/ppermute | solution.py:30
  52.7 8.8 %collective-permute-start.11 = (bf16[8,7168]{1,0:T(8,128)(2,1)S(1)}, bf16[8,7168]{1,0:T(8,128)(2,1)S(1)}, u32[]{:S(2)}, u32[]{:S(2)}) collective-permute-start(bf16[8,7168]{1,0:T(8,128)(2,1)S(1)} %get-tuple-element.15), channel_id=1, source_target_pairs={{0,12},{1,13},{2,14},{3,15},{4,8},{5,9},{6,10},{7,11},{8,4},{9,5},... | collective-permute-start | bytes 344072 | tf_op jit(solution)/shard_map/ppermute | solution.py:30

commit v3 on v2

--- a/solution.py
+++ b/solution.py
@@ -42,14 +42,15 @@
 
 def scatter_sum(even, odd):
     rows = even.shape[0] // (PANELS // 2)
+    fars = range(PANELS // 4 - 1, -1, -1)
     part = (even.astype(f32) + swap(odd, 1).astype(f32)).reshape(PANELS // 2, rows, -1)
-    own = {}
-    for far in range(PANELS // 4 - 1, -1, -1):
-        own[far] = part[2 * far] + swap(part[2 * far + 1].astype(bf16), 2).astype(f32)
-    terms = [own[0]]
-    for far in range(PANELS // 4 - 1, 0, -1):
-        terms.append(swap(own[far].astype(bf16), 4 * far))
-    return terms
+    kept = lax.optimization_barrier([part[2 * far] for far in fars])
+    sent = lax.optimization_barrier([part[2 * far + 1].astype(bf16) for far in fars])
+    terms = []
+    for far, mine, other in zip(fars, kept, sent):
+        own = mine + swap(other, 2).astype(f32)
+        terms.append(swap(own.astype(bf16), 4 * far) if far else own)
+    return terms[::-1]
 
 
 def slot_places(routes, expert):
@@ -71,61 +72,86 @@
     return jnp.sum(place * route_prob, axis=1, keepdims=True)
 
 
-def pick_kernel(experts, routes_ref, probs_ref, tokens_ref, grads_ref, send_ref, place_ref, weight_ref):
-    @pl.when(pl.program_id(0) == 0)
-    def _():
+def pick_kernel(experts, chunk, routes_hbm, probs_hbm, tokens_hbm, grads_hbm, send_ref, *scratch):
+    routes_ref, probs_ref, tokens_ref, grads_ref, small_sems, token_sems, grad_sems = scratch
+    width = tokens_ref.shape[1]
+    starts = range(0, width, chunk)
+    small = [
+        pltpu.make_async_copy(routes_hbm, routes_ref, small_sems.at[0]),
+        pltpu.make_async_copy(probs_hbm, probs_ref, small_sems.at[1]),
+    ]
+    for copy in small:
+        copy.start()
+    large = []
+    for i, start in enumerate(starts):
+        cols = pl.ds(start, chunk)
+        large.append(
+            (
+                pltpu.make_async_copy(tokens_hbm.at[:, cols], tokens_ref.at[:, cols], token_sems.at[i]),
+                pltpu.make_async_copy(grads_hbm.at[:, cols], grads_ref.at[:, cols], grad_sems.at[i]),
+            )
+        )
+        for copy in large[-1]:
+            copy.start()
+    for copy in small:
+        copy.wait()
+    places, weights = [], []
+    for e in range(experts):
+        matches, place = slot_places(routes_ref[...], e)
+        places.append(place.astype(bf16))
+        weights.append(slot_probs(matches, place, probs_ref[...]))
+    for i, start in enumerate(starts):
+        cols = slice(start, start + chunk)
+        for copy in large[i]:
+            copy.wait()
         for e in range(experts):
-            matches, place = slot_places(routes_ref[...], e)
-            place_ref[e] = place.astype(bf16)
-            weight_ref[e] = slot_probs(matches, place, probs_ref[...])
-
-    for e in range(experts):
-        place = place_ref[e]
-        picked = jnp.dot(place, tokens_ref[...], preferred_element_type=f32)
-        grads = jnp.dot(place, grads_ref[...], preferred_element_type=f32)
-        is_token = lax.broadcasted_iota(jnp.int32, picked.shape, 0) < CAP
-        send_ref[e] = jnp.where(is_token, picked, weight_ref[e] * grads).astype(bf16)
+            picked = jnp.dot(places[e], tokens_ref[:, cols], preferred_element_type=f32)
+            grads = jnp.dot(places[e], grads_ref[:, cols], preferred_element_type=f32)
+            is_token = lax.broadcasted_iota(jnp.int32, picked.shape, 0) < CAP
+            send_ref[e, :, cols] = jnp.where(is_token, picked, weights[e] * grads).astype(bf16)
 
 
 def pick(routes, probs, tokens, grads, experts):
     count, width = tokens.shape
     chunk = chunk_of(width, 1792)
     topk = routes.shape[0]
-    whole = lambda i: (0, 0)
+    hbm = pl.BlockSpec(memory_space=pltpu.HBM)
     return pl.pallas_call(
-        functools.partial(pick_kernel, experts),
-        grid=(width // chunk,),
-        in_specs=[
-            pl.BlockSpec((topk, count), whole),
-            pl.BlockSpec((topk, count), whole),
-            pl.BlockSpec((count, chunk), lambda i: (0, i)),
-            pl.BlockSpec((count, chunk), lambda i: (0, i)),
+        functools.partial(pick_kernel, experts, chunk),
+        in_specs=[hbm] * 4,
+        out_specs=pl.BlockSpec(memory_space=pltpu.VMEM),
+        out_shape=jax.ShapeDtypeStruct((experts, PAIR, width), bf16),
+        scratch_shapes=[
+            pltpu.VMEM((topk, count), routes.dtype),
+            pltpu.VMEM((topk, count), probs.dtype),
+            pltpu.VMEM((count, width), bf16),
+            pltpu.VMEM((count, width), bf16),
+            pltpu.SemaphoreType.DMA((2,)),
+            pltpu.SemaphoreType.DMA((width // chunk,)),
+            pltpu.SemaphoreType.DMA((width // chunk,)),
         ],
-        out_specs=pl.BlockSpec((experts, PAIR, chunk), lambda i: (0, 0, i)),
-        out_shape=jax.ShapeDtypeStruct((experts, PAIR, width), bf16),
-        scratch_shapes=[pltpu.VMEM((experts, PAIR, count), bf16), pltpu.VMEM((experts, PAIR, 1), f32)],
         compiler_params=pltpu.CompilerParams(vmem_limit_bytes=16 * MIB),
         cost_estimate=pl.CostEstimate(
             flops=4 * experts * PAIR * count * width, bytes_accessed=4 * count * width, transcendentals=0
         ),
         name="pick_rows",
-    )(routes, probs, tokens, grads)
+    )(*[pltpu.with_memory_space_constraint(x, pltpu.HBM) for x in (routes, probs, tokens, grads)])
 
 
 def expert_kernel(chunk, even_ref, odd_ref, gate_ref, up_ref, down_ref, even_out, odd_out):
     half, width = even_ref.shape
     count = 2 * half
     units = down_ref.shape[0]
-    gate_pre = jnp.zeros((count, units), f32)
-    up_pre = jnp.zeros((count, units), f32)
+    both_pre = jnp.zeros((count, 2 * units), f32)
     hidden_grad = jnp.zeros((count, units), f32)
     for start in range(0, width, chunk):
         cols = slice(start, start + chunk)
         rows = jnp.concatenate([even_ref[:, cols], odd_ref[:, cols]], axis=0)
-        gate_pre += jnp.dot(rows, gate_ref[cols, :], preferred_element_type=f32)
-        up_pre += jnp.dot(rows, up_ref[cols, :], preferred_element_type=f32)
+        both = jnp.concatenate([gate_ref[cols, :], up_ref[cols, :]], axis=1)
+        both_pre += jnp.dot(rows, both, preferred_element_type=f32)
         hidden_grad += lax.dot_general(rows, down_ref[:, cols], NT, preferred_element_type=f32)
     is_token = lax.broadcasted_iota(jnp.int32, (count, units), 0) % PAIR < CAP
+    gate_pre, up_pre = both_pre[:, :units], both_pre[:, units:]
     hidden_grad = pltpu.roll(hidden_grad, count - CAP, 0)
     sigmoid_gate = jax.nn.sigmoid(gate_pre)
     silu_gate = gate_pre * sigmoid_gate
@@ -136,11 +162,12 @@
     hidden = jnp.where(is_token, hidden, 0.0).astype(bf16)
     gate_grad = jnp.where(is_token, 0.0, gate_grad).astype(bf16)
     up_grad = jnp.where(is_token, 0.0, up_grad).astype(bf16)
+    both_grad = jnp.concatenate([gate_grad, up_grad], axis=1)
     for start in range(0, width, chunk):
         cols = slice(start, start + chunk)
         part = jnp.dot(hidden, down_ref[:, cols], preferred_element_type=f32)
-        part += lax.dot_general(gate_grad, gate_ref[cols, :], NT, preferred_element_type=f32)
-        part += lax.dot_general(up_grad, up_ref[cols, :], NT, preferred_element_type=f32)
+        both = jnp.concatenate([gate_ref[cols, :], up_ref[cols, :]], axis=1)
+        part += lax.dot_general(both_grad, both, NT, preferred_element_type=f32)
         part = part.astype(bf16)
         even_out[:, cols] = part[:half]
         odd_out[:, cols] = part[half:]

time: 65.9 us -> 59.4 us (0.901)
  local copies, waits for them, and re-layouts: 4.51 us -> 0.2 us
  waiting for transfers between devices: 30.8 us -> 28.1 us
  Pallas kernels: 9.11 us -> 9.98 us
    unnamed x29 -> x21, local copies, waits for them, and re-layouts: 4.47 us -> 0.09 us
    ppermute x16, waiting for transfers between devices: 30.8 us -> 28.1 us  [swap(): return lax.ppermute(x, AXIS, [(i, i ^ offset) for i in range(devices)])]
    pallas_call x1, Pallas kernels: 1.42 us -> 2.95 us  [pick(): pl.pallas_call(functools.partial(pick_kernel, experts, chunk), in_specs=[...]
  transfers between devices with their start and end apart: 16 -> 16, of which waited for: 11 -> 9; matrix products, arithmetic and copies ran while one was open for 0% -> 0% of each run, Pallas kernels for 0% -> 0%
where the time goes in v3:
time: 59.4 us; the launch traced here: 59.3 us
  waiting for transfers between devices  28.1 us (47%)
  starting transfers between devices  19.8 us (33%)
  Pallas kernels  9.98 us (17%)
  between operations  0.83 us (1%)
    ppermute x16, waiting for transfers between devices, swap(): return lax.ppermute(x, AXIS, [(i, i ^ offset) for i in range(devices)])  28.1 us
    ppermute x16, starting transfers between devices, swap(): return lax.ppermute(x, AXIS, [(i, i ^ offset) for i in range(devices)])  19.8 us
    pallas_call x1, Pallas kernels, finish(): pl.pallas_call(functools.partial(finish_kernel, experts, len(terms)), gri...  4.13 us
    pallas_call x1, Pallas kernels, pick(): pl.pallas_call(functools.partial(pick_kernel, experts, chunk), in_specs=[...  2.95 us
    pallas_call x1, Pallas kernels, expert_rows(): pl.pallas_call(functools.partial(expert_kernel, chunk_of(width, 1024)), i...  2.91 us
  transfers between devices with their start and end apart: 16, of which 9 were waited for; matrix products, arithmetic and copies ran while one was open for 0% of the time, Pallas kernels for 0%

profile of v3, /device:TPU:0, one launch (start us, length us, event | category | flops | bytes accessed | tf_op | source)
XLA Modules:
  0.0 59.3 jit_solution(7501814669285136636)
XLA Ops:
  0.7 2.9 %pick_rows.1 = bf16[1,8,7168]{2,1,0:T(8,128)(2,1)S(1)} custom-call(s32[8,128]{1,0:T(8,128)} %bitcast.17, f32[8,128]{1,0:T(8,128)} %bitcast.19, bf16[128,7168]{1,0:T(8,128)(2,1)} %tokens_ref.1, bf16[128,7168]{1,0:T(8,128)(2,1)} %grads_ref.1), custom_call_target="tpu_custom_call" | custom-call | flops 29360128 | bytes 3670016 | tf_op jit(solution)/shard_map/pick_rows/pallas_call | solution.py:119
  3.6 0.0 copy-start.2
  3.6 5.1 %collective-permute-start.5 = (bf16[8,7168]{1,0:T(8,128)(2,1)S(1)}, bf16[8,7168]{1,0:T(8,128)(2,1)S(1)}, u32[]{:S(2)}, u32[]{:S(2)}) collective-permute-start(bf16[8,7168]{1,0:T(8,128)(2,1)S(1)} %bitcast.10), channel_id=1, source_target_pairs={{0,12},{1,13},{2,14},{3,15},{4,8},{5,9},{6,10},{7,11},{8,4},{9,5},... | collective-permute-start | bytes 344072 | tf_op jit(solution)/shard_map/ppermute | solution.py:30
  8.7 0.6 %collective-permute-start.1 = (bf16[8,7168]{1,0:T(8,128)(2,1)S(1)}, bf16[8,7168]{1,0:T(8,128)(2,1)S(1)}, u32[]{:S(2)}, u32[]{:S(2)}) collective-permute-start(bf16[8,7168]{1,0:T(8,128)(2,1)S(1)} %bitcast.12), channel_id=1, source_target_pairs={{0,4},{1,5},{2,6},{3,7},{4,0},{5,1},{6,2},{7,3},{8,12},{9,13},{10,... | collective-permute-start | bytes 344072 | tf_op jit(solution)/shard_map/ppermute | solution.py:30
  9.4 1.7 %collective-permute-start = (bf16[8,7168]{1,0:T(8,128)(2,1)S(1)}, bf16[8,7168]{1,0:T(8,128)(2,1)S(1)}, u32[]{:S(2)}, u32[]{:S(2)}) collective-permute-start(bf16[8,7168]{1,0:T(8,128)(2,1)S(1)} %bitcast.13), channel_id=1, source_target_pairs={{0,2},{1,3},{2,0},{3,1},{4,6},{5,7},{6,4},{7,5},{8,10},{9,11},{10,... | collective-permute-start | bytes 344072 | tf_op jit(solution)/shard_map/ppermute | solution.py:30
  11.1 1.8 %collective-permute-done.5 = bf16[8,7168]{1,0:T(8,128)(2,1)S(1)} collective-permute-done((bf16[8,7168]{1,0:T(8,128)(2,1)S(1)}, bf16[8,7168]{1,0:T(8,128)(2,1)S(1)}, u32[]{:S(2)}, u32[]{:S(2)}) %collective-permute-start.5) | collective-permute-done | bytes 114720 | tf_op jit(solution)/shard_map/ppermute | solution.py:30
  12.8 1.7 %collective-permute-start.6 = (bf16[8,7168]{1,0:T(8,128)(2,1)S(1)}, bf16[8,7168]{1,0:T(8,128)(2,1)S(1)}, u32[]{:S(2)}, u32[]{:S(2)}) collective-permute-start(bf16[8,7168]{1,0:T(8,128)(2,1)S(1)} %collective-permute-done.5), channel_id=1, source_target_pairs={{0,2},{1,3},{2,0},{3,1},{4,6},{5,7},{6,4},{7,5},{8,10},{9,11},{10,... | collective-permute-start | bytes 344072 | tf_op jit(solution)/shard_map/ppermute | solution.py:30
  14.5 3.9 %collective-permute-done.3 = bf16[8,7168]{1,0:T(8,128)(2,1)S(1)} collective-permute-done((bf16[8,7168]{1,0:T(8,128)(2,1)S(1)}, bf16[8,7168]{1,0:T(8,128)(2,1)S(1)}, u32[]{:S(2)}, u32[]{:S(2)}) %collective-permute-start.3) | collective-permute-done | bytes 114720 | tf_op jit(solution)/shard_map/ppermute | solution.py:30
  18.4 1.5 %collective-permute-start.4 = (bf16[8,7168]{1,0:T(8,128)(2,1)S(1)}, bf16[8,7168]{1,0:T(8,128)(2,1)S(1)}, u32[]{:S(2)}, u32[]{:S(2)}) collective-permute-start(bf16[8,7168]{1,0:T(8,128)(2,1)S(1)} %collective-permute-done.3), channel_id=1, source_target_pairs={{0,2},{1,3},{2,0},{3,1},{4,6},{5,7},{6,4},{7,5},{8,10},{9,11},{10,... | collective-permute-start | bytes 344072 | tf_op jit(solution)/shard_map/ppermute | solution.py:30
  19.9 0.5 collective-permute-start.2
  20.5 0.0 collective-permute-done
  20.5 4.6 %collective-permute-done.2 = bf16[8,7168]{1,0:T(8,128)(2,1)S(1)} collective-permute-done((bf16[8,7168]{1,0:T(8,128)(2,1)S(1)}, bf16[8,7168]{1,0:T(8,128)(2,1)S(1)}, u32[]{:S(2)}, u32[]{:S(2)}) %collective-permute-start.2) | collective-permute-done | bytes 114720 | tf_op jit(solution)/shard_map/ppermute | solution.py:30
  25.1 0.0 collective-permute-done.4
  25.2 0.1 collective-permute-start.7
  25.3 2.5 %collective-permute-done.7.odd_ref = bf16[64,7168]{1,0:T(8,128)(2,1)S(1)} collective-permute-done((bf16[64,7168]{1,0:T(8,128)(2,1)S(1)}, bf16[64,7168]{1,0:T(8,128)(2,1)S(1)}, u32[]{:S(2)}, u32[]{:S(2)}) %collective-permute-start.7) | collective-permute-done | bytes 917536 | tf_op jit(solution)/shard_map/ppermute | solution.py:30
  27.7 2.9 %expert_rows.1 = (bf16[64,7168]{1,0:T(8,128)(2,1)S(1)}, bf16[64,7168]{1,0:T(8,128)(2,1)S(1)}) custom-call(bf16[64,7168]{1,0:T(8,128)(2,1)S(1)} %constant_dynamic-update-slice_fusion.even_ref, bf16[64,7168]{1,0:T(8,128)(2,1)S(1)} %collective-permute-done.7.odd_ref, bf16[7168,128]{1,0:T(8,128)(2,1)S(1)} %copy-done.2, bf16[7168,128]{1,0:T(8,128)(2,1)S(1)} %copy-done.3, ...), custom_call_target="tpu_custom_call" | custom-call | flops 1409286144 | bytes 9175040 | tf_op jit(solution)/shard_map/expert_rows/pallas_call | solution.py:180
  30.6 0.2 collective-permute-start.8
  30.8 2.3 %collective-permute-done.8 = bf16[64,7168]{1,0:T(8,128)(2,1)S(1)} collective-permute-done((bf16[64,7168]{1,0:T(8,128)(2,1)S(1)}, bf16[64,7168]{1,0:T(8,128)(2,1)S(1)}, u32[]{:S(2)}, u32[]{:S(2)}) %collective-permute-start.8) | collective-permute-done | bytes 917536 | tf_op jit(solution)/shard_map/ppermute | solution.py:30
  33.2 0.2 fusion
  33.5 1.6 %collective-permute-start.9 = (bf16[8,7168]{1,0:T(8,128)(2,1)S(1)}, bf16[8,7168]{1,0:T(8,128)(2,1)S(1)}, u32[]{:S(2)}, u32[]{:S(2)}) collective-permute-start(bf16[8,7168]{1,0:T(8,128)(2,1)S(1)} %get-tuple-element.19), channel_id=1, source_target_pairs={{0,2},{1,3},{2,0},{3,1},{4,6},{5,7},{6,4},{7,5},{8,10},{9,11},{10,... | collective-permute-start | bytes 344072 | tf_op jit(solution)/shard_map/ppermute | solution.py:30
  35.1 0.5 collective-permute-start.10
  35.6 1.5 %collective-permute-start.12 = (bf16[8,7168]{1,0:T(8,128)(2,1)S(1)}, bf16[8,7168]{1,0:T(8,128)(2,1)S(1)}, u32[]{:S(2)}, u32[]{:S(2)}) collective-permute-start(bf16[8,7168]{1,0:T(8,128)(2,1)S(1)} %get-tuple-element.23), channel_id=1, source_target_pairs={{0,2},{1,3},{2,0},{3,1},{4,6},{5,7},{6,4},{7,5},{8,10},{9,11},{10,... | collective-permute-start | bytes 344072 | tf_op jit(solution)/shard_map/ppermute | solution.py:30
  37.1 0.5 collective-permute-start.14
  37.6 0.1 fusion.1
  37.7 4.3 %collective-permute-done.10 = bf16[8,7168]{1,0:T(8,128)(2,1)S(1)} collective-permute-done((bf16[8,7168]{1,0:T(8,128)(2,1)S(1)}, bf16[8,7168]{1,0:T(8,128)(2,1)S(1)}, u32[]{:S(2)}, u32[]{:S(2)}) %collective-permute-start.10) | collective-permute-done | bytes 114720 | tf_op jit(solution)/shard_map/ppermute | solution.py:30
  42.0 0.6 %collective-permute-start.11 = (bf16[8,7168]{1,0:T(8,128)(2,1)S(1)}, bf16[8,7168]{1,0:T(8,128)(2,1)S(1)}, u32[]{:S(2)}, u32[]{:S(2)}) collective-permute-start(bf16[8,7168]{1,0:T(8,128)(2,1)S(1)} %add_convert_fusion.2), channel_id=1, source_target_pairs={{0,4},{1,5},{2,6},{3,7},{4,0},{5,1},{6,2},{7,3},{8,12},{9,13},{10,... | collective-permute-start | bytes 344072 | tf_op jit(solution)/shard_map/ppermute | solution.py:30
  42.7 1.8 %collective-permute-done.12 = bf16[8,7168]{1,0:T(8,128)(2,1)S(1)} collective-permute-done((bf16[8,7168]{1,0:T(8,128)(2,1)S(1)}, bf16[8,7168]{1,0:T(8,128)(2,1)S(1)}, u32[]{:S(2)}, u32[]{:S(2)}) %collective-permute-start.12) | collective-permute-done | bytes 114720 | tf_op jit(solution)/shard_map/ppermute | solution.py:30
  44.5 1.2 %collective-permute-start.13 = (bf16[8,7168]{1,0:T(8,128)(2,1)S(1)}, bf16[8,7168]{1,0:T(8,128)(2,1)S(1)}, u32[]{:S(2)}, u32[]{:S(2)}) collective-permute-start(bf16[8,7168]{1,0:T(8,128)(2,1)S(1)} %add_convert_fusion.1), channel_id=1, source_target_pairs={{0,8},{1,9},{2,10},{3,11},{4,12},{5,13},{6,14},{7,15},{8,0},{9,1},... | collective-permute-start | bytes 344072 | tf_op jit(solution)/shard_map/ppermute | solution.py:30
  45.7 0.4 collective-permute-done.14
  46.1 2.4 %collective-permute-start.15 = (bf16[8,7168]{1,0:T(8,128)(2,1)S(1)}, bf16[8,7168]{1,0:T(8,128)(2,1)S(1)}, u32[]{:S(2)}, u32[]{:S(2)}) collective-permute-start(bf16[8,7168]{1,0:T(8,128)(2,1)S(1)} %add_convert_fusion), channel_id=1, source_target_pairs={{0,12},{1,13},{2,14},{3,15},{4,8},{5,9},{6,10},{7,11},{8,4},{9,5},... | collective-permute-start | bytes 344072 | tf_op jit(solution)/shard_map/ppermute | solution.py:30
  48.5 6.6 %collective-permute-done.13 = bf16[8,7168]{1,0:T(8,128)(2,1)S(1)} collective-permute-done((bf16[8,7168]{1,0:T(8,128)(2,1)S(1)}, bf16[8,7168]{1,0:T(8,128)(2,1)S(1)}, u32[]{:S(2)}, u32[]{:S(2)}) %collective-permute-start.13) | collective-permute-done | bytes 114720 | tf_op jit(solution)/shard_map/ppermute | solution.py:30
  55.2 4.1 %finish.1 = (bf16[128,7168]{1,0:T(8,128)(2,1)}, bf16[128,7168]{1,0:T(8,128)(2,1)}, f32[8,128]{1,0:T(8,128)}) custom-call(s32[8,128]{1,0:T(8,128)S(1)} %bitcast.18, f32[8,128]{1,0:T(8,128)S(1)} %bitcast.20, bf16[128,7168]{1,0:T(8,128)(2,1)S(1)} %copy-done, bf16[128,7168]{1,0:T(8,128)(2,1)S(1)} %copy-done.1, f32[1,8,7168]{2,1,0:T(8,128)S(1)} %add_bitcast_fusion.refs_0_, ...), custom_call_target="tpu_custom_call" | custom-call | flops 117440512 | bytes 7340032 | tf_op jit(solution)/shard_map/finish/pallas_call | solution.py:258
  (32 shorter events, 0.2 us)
Async XLA Ops:
  0.6 27.1 %copy-start.3 = (bf16[7168,128]{1,0:T(8,128)(2,1)S(1)}, bf16[7168,128]{1,0:T(8,128)(2,1)}, u32[]{:S(2)}) copy-start(bf16[7168,128]{1,0:T(8,128)(2,1)} %up_ref.1) | copy-start | bytes 5505028
  0.6 27.1 %copy-start.4 = (bf16[128,7168]{1,0:T(8,128)(2,1)S(1)}, bf16[128,7168]{1,0:T(8,128)(2,1)}, u32[]{:S(2)}) copy-start(bf16[128,7168]{1,0:T(8,128)(2,1)} %down_ref.1) | copy-start | bytes 5505028
  3.6 24.1 %copy-start.2 = (bf16[7168,128]{1,0:T(8,128)(2,1)S(1)}, bf16[7168,128]{1,0:T(8,128)(2,1)}, u32[]{:S(2)}) copy-start(bf16[7168,128]{1,0:T(8,128)(2,1)} %gate_ref.1) | copy-start | bytes 5505028
  3.6 9.2 %collective-permute-start.5 = (bf16[8,7168]{1,0:T(8,128)(2,1)S(1)}, bf16[8,7168]{1,0:T(8,128)(2,1)S(1)}, u32[]{:S(2)}, u32[]{:S(2)}) collective-permute-start(bf16[8,7168]{1,0:T(8,128)(2,1)S(1)} %bitcast.10), channel_id=1, source_target_pairs={{0,12},{1,13},{2,14},{3,15},{4,8},{5,9},{6,10},{7,11},{8,4},{9,5},... | collective-permute-start | bytes 344072 | tf_op jit(solution)/shard_map/ppermute | solution.py:30
  8.7 9.7 %collective-permute-start.3 = (bf16[8,7168]{1,0:T(8,128)(2,1)S(1)}, bf16[8,7168]{1,0:T(8,128)(2,1)S(1)}, u32[]{:S(2)}, u32[]{:S(2)}) collective-permute-start(bf16[8,7168]{1,0:T(8,128)(2,1)S(1)} %bitcast.11), channel_id=1, source_target_pairs={{0,8},{1,9},{2,10},{3,11},{4,12},{5,13},{6,14},{7,15},{8,0},{9,1},... | collective-permute-start | bytes 344072 | tf_op jit(solution)/shard_map/ppermute | solution.py:30
  8.7 11.2 %collective-permute-start.1 = (bf16[8,7168]{1,0:T(8,128)(2,1)S(1)}, bf16[8,7168]{1,0:T(8,128)(2,1)S(1)}, u32[]{:S(2)}, u32[]{:S(2)}) collective-permute-start(bf16[8,7168]{1,0:T(8,128)(2,1)S(1)} %bitcast.12), channel_id=1, source_target_pairs={{0,4},{1,5},{2,6},{3,7},{4,0},{5,1},{6,2},{7,3},{8,12},{9,13},{10,... | collective-permute-start | bytes 344072 | tf_op jit(solution)/shard_map/ppermute | solution.py:30
  9.4 11.1 %collective-permute-start = (bf16[8,7168]{1,0:T(8,128)(2,1)S(1)}, bf16[8,7168]{1,0:T(8,128)(2,1)S(1)}, u32[]{:S(2)}, u32[]{:S(2)}) collective-permute-start(bf16[8,7168]{1,0:T(8,128)(2,1)S(1)} %bitcast.13), channel_id=1, source_target_pairs={{0,2},{1,3},{2,0},{3,1},{4,6},{5,7},{6,4},{7,5},{8,10},{9,11},{10,... | collective-permute-start | bytes 344072 | tf_op jit(solution)/shard_map/ppermute | solution.py:30
  12.8 12.3 %collective-permute-start.6 = (bf16[8,7168]{1,0:T(8,128)(2,1)S(1)}, bf16[8,7168]{1,0:T(8,128)(2,1)S(1)}, u32[]{:S(2)}, u32[]{:S(2)}) collective-permute-start(bf16[8,7168]{1,0:T(8,128)(2,1)S(1)} %collective-permute-done.5), channel_id=1, source_target_pairs={{0,2},{1,3},{2,0},{3,1},{4,6},{5,7},{6,4},{7,5},{8,10},{9,11},{10,... | collective-permute-start | bytes 344072 | tf_op jit(solution)/shard_map/ppermute | solution.py:30
  18.4 6.7 %collective-permute-start.4 = (bf16[8,7168]{1,0:T(8,128)(2,1)S(1)}, bf16[8,7168]{1,0:T(8,128)(2,1)S(1)}, u32[]{:S(2)}, u32[]{:S(2)}) collective-permute-start(bf16[8,7168]{1,0:T(8,128)(2,1)S(1)} %collective-permute-done.3), channel_id=1, source_target_pairs={{0,2},{1,3},{2,0},{3,1},{4,6},{5,7},{6,4},{7,5},{8,10},{9,11},{10,... | collective-permute-start | bytes 344072 | tf_op jit(solution)/shard_map/ppermute | solution.py:30
  19.9 5.2 %collective-permute-start.2 = (bf16[8,7168]{1,0:T(8,128)(2,1)S(1)}, bf16[8,7168]{1,0:T(8,128)(2,1)S(1)}, u32[]{:S(2)}, u32[]{:S(2)}) collective-permute-start(bf16[8,7168]{1,0:T(8,128)(2,1)S(1)} %collective-permute-done.1), channel_id=1, source_target_pairs={{0,2},{1,3},{2,0},{3,1},{4,6},{5,7},{6,4},{7,5},{8,10},{9,11},{10,... | collective-permute-start | bytes 344072 | tf_op jit(solution)/shard_map/ppermute | solution.py:30
  25.2 2.5 %collective-permute-start.7 = (bf16[64,7168]{1,0:T(8,128)(2,1)S(1)}, bf16[64,7168]{1,0:T(8,128)(2,1)S(1)}, u32[]{:S(2)}, u32[]{:S(2)}) collective-permute-start(bf16[64,7168]{1,0:T(8,128)(2,1)S(1)} %constant_dynamic-update-slice_fusion.even_ref), channel_id=1, source_target_pairs={{0,1},{1,0},{2,3},{3,2},{4,5},{5,4},{6,7},{7,6},{8,9},{9,8},{10,11... | collective-permute-start | bytes 2752520 | tf_op jit(solution)/shard_map/ppermute | solution.py:30
  30.6 2.5 %collective-permute-start.8 = (bf16[64,7168]{1,0:T(8,128)(2,1)S(1)}, bf16[64,7168]{1,0:T(8,128)(2,1)S(1)}, u32[]{:S(2)}, u32[]{:S(2)}) collective-permute-start(bf16[64,7168]{1,0:T(8,128)(2,1)S(1)} %get-tuple-element.17), channel_id=1, source_target_pairs={{0,1},{1,0},{2,3},{3,2},{4,5},{5,4},{6,7},{7,6},{8,9},{9,8},{10,11... | collective-permute-start | bytes 2752520 | tf_op jit(solution)/shard_map/ppermute | solution.py:30
  33.5 15.0 %collective-permute-start.9 = (bf16[8,7168]{1,0:T(8,128)(2,1)S(1)}, bf16[8,7168]{1,0:T(8,128)(2,1)S(1)}, u32[]{:S(2)}, u32[]{:S(2)}) collective-permute-start(bf16[8,7168]{1,0:T(8,128)(2,1)S(1)} %get-tuple-element.19), channel_id=1, source_target_pairs={{0,2},{1,3},{2,0},{3,1},{4,6},{5,7},{6,4},{7,5},{8,10},{9,11},{10,... | collective-permute-start | bytes 344072 | tf_op jit(solution)/shard_map/ppermute | solution.py:30
  35.1 6.9 %collective-permute-start.10 = (bf16[8,7168]{1,0:T(8,128)(2,1)S(1)}, bf16[8,7168]{1,0:T(8,128)(2,1)S(1)}, u32[]{:S(2)}, u32[]{:S(2)}) collective-permute-start(bf16[8,7168]{1,0:T(8,128)(2,1)S(1)} %get-tuple-element.21), channel_id=1, source_target_pairs={{0,2},{1,3},{2,0},{3,1},{4,6},{5,7},{6,4},{7,5},{8,10},{9,11},{10,... | collective-permute-start | bytes 344072 | tf_op jit(solution)/shard_map/ppermute | solution.py:30
  35.6 8.9 %collective-permute-start.12 = (bf16[8,7168]{1,0:T(8,128)(2,1)S(1)}, bf16[8,7168]{1,0:T(8,128)(2,1)S(1)}, u32[]{:S(2)}, u32[]{:S(2)}) collective-permute-start(bf16[8,7168]{1,0:T(8,128)(2,1)S(1)} %get-tuple-element.23), channel_id=1, source_target_pairs={{0,2},{1,3},{2,0},{3,1},{4,6},{5,7},{6,4},{7,5},{8,10},{9,11},{10,... | collective-permute-start | bytes 344072 | tf_op jit(solution)/shard_map/ppermute | solution.py:30
  37.1 9.0 %collective-permute-start.14 = (bf16[8,7168]{1,0:T(8,128)(2,1)S(1)}, bf16[8,7168]{1,0:T(8,128)(2,1)S(1)}, u32[]{:S(2)}, u32[]{:S(2)}) collective-permute-start(bf16[8,7168]{1,0:T(8,128)(2,1)S(1)} %get-tuple-element.25), channel_id=1, source_target_pairs={{0,2},{1,3},{2,0},{3,1},{4,6},{5,7},{6,4},{7,5},{8,10},{9,11},{10,... | collective-permute-start | bytes 344072 | tf_op jit(solution)/shard_map/ppermute | solution.py:30
  37.6 17.5 %copy-start = (bf16[128,7168]{1,0:T(8,128)(2,1)S(1)}, bf16[128,7168]{1,0:T(8,128)(2,1)}, u32[]{:S(2)}) copy-start(bf16[128,7168]{1,0:T(8,128)(2,1)} %tokens_ref.1) | copy-start | bytes 5505028
  37.6 17.6 %copy-start.1 = (bf16[128,7168]{1,0:T(8,128)(2,1)S(1)}, bf16[128,7168]{1,0:T(8,128)(2,1)}, u32[]{:S(2)}) copy-start(bf16[128,7168]{1,0:T(8,128)(2,1)} %grads_ref.1) | copy-start | bytes 5505028
  37.6 17.6 %copy-start.5 = (s32[128,8]{0,1:T(8,128)S(1)}, s32[128,8]{0,1:T(8,128)}, u32[]{:S(2)}) copy-start(s32[128,8]{0,1:T(8,128)} %param.9) | copy-start | bytes 12292
  37.6 17.6 %copy-start.6 = (f32[128,8]{0,1:T(8,128)S(1)}, f32[128,8]{0,1:T(8,128)}, u32[]{:S(2)}) copy-start(f32[128,8]{0,1:T(8,128)} %param.10) | copy-start | bytes 12292
  42.0 6.5 %collective-permute-start.11 = (bf16[8,7168]{1,0:T(8,128)(2,1)S(1)}, bf16[8,7168]{1,0:T(8,128)(2,1)S(1)}, u32[]{:S(2)}, u32[]{:S(2)}) collective-permute-start(bf16[8,7168]{1,0:T(8,128)(2,1)S(1)} %add_convert_fusion.2), channel_id=1, source_target_pairs={{0,4},{1,5},{2,6},{3,7},{4,0},{5,1},{6,2},{7,3},{8,12},{9,13},{10,... | collective-permute-start | bytes 344072 | tf_op jit(solution)/shard_map/ppermute | solution.py:30
  44.5 10.7 %collective-permute-start.13 = (bf16[8,7168]{1,0:T(8,128)(2,1)S(1)}, bf16[8,7168]{1,0:T(8,128)(2,1)S(1)}, u32[]{:S(2)}, u32[]{:S(2)}) collective-permute-start(bf16[8,7168]{1,0:T(8,128)(2,1)S(1)} %add_convert_fusion.1), channel_id=1, source_target_pairs={{0,8},{1,9},{2,10},{3,11},{4,12},{5,13},{6,14},{7,15},{8,0},{9,1},... | collective-permute-start | bytes 344072 | tf_op jit(solution)/shard_map/ppermute | solution.py:30
  46.1 9.0 %collective-permute-start.15 = (bf16[8,7168]{1,0:T(8,128)(2,1)S(1)}, bf16[8,7168]{1,0:T(8,128)(2,1)S(1)}, u32[]{:S(2)}, u32[]{:S(2)}) collective-permute-start(bf16[8,7168]{1,0:T(8,128)(2,1)S(1)} %add_convert_fusion), channel_id=1, source_target_pairs={{0,12},{1,13},{2,14},{3,15},{4,8},{5,9},{6,10},{7,11},{8,4},{9,5},... | collective-permute-start | bytes 344072 | tf_op jit(solution)/shard_map/ppermute | solution.py:30

commit v4 on v3

--- a/solution.py
+++ b/solution.py
@@ -14,6 +14,8 @@
 PAIR = 2 * CAP
 AXIS = "expert"
 MIB = 1 << 20
+VMEM = pl.BlockSpec(memory_space=pltpu.VMEM)
+ANY = pl.BlockSpec(memory_space=pl.ANY)
 
 f32 = jnp.float32
 bf16 = jnp.bfloat16
@@ -30,27 +32,31 @@
     return lax.ppermute(x, AXIS, [(i, i ^ offset) for i in range(devices)])
 
 
-def gather_rows(x):
-    blocks = {0: x}
-    for far in range(PANELS // 4 - 1, 0, -1):
-        blocks[4 * far] = swap(x, 4 * far)
-    for far in range(PANELS // 4):
-        blocks[4 * far + 2] = swap(blocks[4 * far], 2)
-    even = jnp.concatenate([blocks[k] for k in range(0, PANELS, 2)], axis=0)
-    return even, swap(even, 1)
-
-
-def scatter_sum(even, odd):
-    rows = even.shape[0] // (PANELS // 2)
-    fars = range(PANELS // 4 - 1, -1, -1)
-    part = (even.astype(f32) + swap(odd, 1).astype(f32)).reshape(PANELS // 2, rows, -1)
-    kept = lax.optimization_barrier([part[2 * far] for far in fars])
-    sent = lax.optimization_barrier([part[2 * far + 1].astype(bf16) for far in fars])
-    terms = []
-    for far, mine, other in zip(fars, kept, sent):
-        own = mine + swap(other, 2).astype(f32)
-        terms.append(swap(own.astype(bf16), 4 * far) if far else own)
-    return terms[::-1]
+NEAR = (0, 2, 4, 6)
+FAR = 8
+
+
+def stack_kernel(chunk, count, *refs):
+    block_refs, out_ref = refs[:count], refs[-1]
+    for start in range(0, out_ref.shape[1], chunk):
+        cols = slice(start, start + chunk)
+        blocks = [ref[:, cols].astype(f32) for ref in block_refs]
+        out_ref[:, cols] = jnp.concatenate(blocks, axis=0).astype(bf16)
+
+
+def stack_rows(blocks, *after):
+    rows, width = blocks[0].shape
+    return pl.pallas_call(
+        functools.partial(stack_kernel, chunk_of(width, 1024), len(blocks)),
+        in_specs=[VMEM] * len(blocks) + [ANY] * len(after),
+        out_specs=VMEM,
+        out_shape=jax.ShapeDtypeStruct((len(blocks) * rows, width), bf16),
+        compiler_params=pltpu.CompilerParams(vmem_limit_bytes=16 * MIB),
+        cost_estimate=pl.CostEstimate(
+            flops=0, bytes_accessed=4 * len(blocks) * rows * width, transcendentals=0
+        ),
+        name="stack_rows",
+    )(*blocks, *after)
 
 
 def slot_places(routes, expert):
@@ -138,15 +144,16 @@
     )(*[pltpu.with_memory_space_constraint(x, pltpu.HBM) for x in (routes, probs, tokens, grads)])
 
 
-def expert_kernel(chunk, even_ref, odd_ref, gate_ref, up_ref, down_ref, even_out, odd_out):
-    half, width = even_ref.shape
+def hidden_rows(chunk, row_refs, gate_ref, up_ref, down_ref):
+    half, width = row_refs[0].shape
+    parts = slice(0, half // 2), slice(half // 2, half)
     count = 2 * half
     units = down_ref.shape[0]
     both_pre = jnp.zeros((count, 2 * units), f32)
     hidden_grad = jnp.zeros((count, units), f32)
     for start in range(0, width, chunk):
         cols = slice(start, start + chunk)
-        rows = jnp.concatenate([even_ref[:, cols], odd_ref[:, cols]], axis=0)
+        rows = jnp.concatenate([ref[part, cols] for part in parts for ref in row_refs], axis=0)
         both = jnp.concatenate([gate_ref[cols, :], up_ref[cols, :]], axis=1)
         both_pre += jnp.dot(rows, both, preferred_element_type=f32)
         hidden_grad += lax.dot_general(rows, down_ref[:, cols], NT, preferred_element_type=f32)
@@ -162,34 +169,112 @@
     hidden = jnp.where(is_token, hidden, 0.0).astype(bf16)
     gate_grad = jnp.where(is_token, 0.0, gate_grad).astype(bf16)
     up_grad = jnp.where(is_token, 0.0, up_grad).astype(bf16)
-    both_grad = jnp.concatenate([gate_grad, up_grad], axis=1)
+    return hidden, jnp.concatenate([gate_grad, up_grad], axis=1)
+
+
+def panel_rows(chunk, hidden, both_grad, gate_ref, up_ref, down_ref, even_out, odd_out):
+    half, width = even_out.shape
     for start in range(0, width, chunk):
         cols = slice(start, start + chunk)
         part = jnp.dot(hidden, down_ref[:, cols], preferred_element_type=f32)
         both = jnp.concatenate([gate_ref[cols, :], up_ref[cols, :]], axis=1)
         part += lax.dot_general(both_grad, both, NT, preferred_element_type=f32)
-        part = part.astype(bf16)
+        odd_out[:, cols] = part[half:].astype(bf16)
         even_out[:, cols] = part[:half]
-        odd_out[:, cols] = part[half:]
-
-
-def expert_rows(even, odd, w_gate, w_up, w_down):
-    half, width = even.shape
-    units = w_down.shape[0]
-    vmem = pl.BlockSpec(memory_space=pltpu.VMEM)
-    return pl.pallas_call(
-        functools.partial(expert_kernel, chunk_of(width, 1024)),
-        in_specs=[vmem] * 5,
-        out_specs=[vmem] * 2,
-        out_shape=[jax.ShapeDtypeStruct((half, width), bf16)] * 2,
-        compiler_params=pltpu.CompilerParams(vmem_limit_bytes=40 * MIB),
+
+
+def first_kernel(chunk, *refs):
+    even_ref, odd_ref, gate_ref, up_ref, down_ref, even_out, odd_out, hidden_out, both_out = refs
+    hidden, both_grad = hidden_rows(chunk, (even_ref, odd_ref), gate_ref, up_ref, down_ref)
+    far = hidden.shape[0] // 2
+    hidden_out[...], both_out[...] = hidden[far:], both_grad[far:]
+    panel_rows(chunk, hidden[:far], both_grad[:far], gate_ref, up_ref, down_ref, even_out, odd_out)
+
+
+def second_kernel(chunk, hidden_ref, both_ref, gate_ref, up_ref, down_ref, even_out, odd_out):
+    panel_rows(chunk, hidden_ref[...], both_ref[...], gate_ref, up_ref, down_ref, even_out, odd_out)
+
+
+def expert_call(kernel, name, operands, out_shape, flops):
+    return pl.pallas_call(
+        functools.partial(kernel, chunk_of(out_shape[0].shape[1], 1024)),
+        in_specs=[VMEM] * len(operands),
+        out_specs=[VMEM] * len(out_shape),
+        out_shape=out_shape,
+        compiler_params=pltpu.CompilerParams(vmem_limit_bytes=24 * MIB),
         cost_estimate=pl.CostEstimate(
-            flops=24 * half * width * units,
-            bytes_accessed=6 * width * units + 8 * half * width,
-            transcendentals=2 * half * units,
+            flops=flops, bytes_accessed=sum(2 * x.size for x in operands), transcendentals=0
         ),
-        name="expert_rows",
-    )(even, odd, w_gate, w_up, w_down)
+        name=name,
+    )(*operands)
+
+
+def expert_far(even, odd, weights):
+    count, width = even.shape
+    units = weights[2].shape[0]
+    out_shape = [
+        jax.ShapeDtypeStruct((count // 2, width), f32),
+        jax.ShapeDtypeStruct((count // 2, width), bf16),
+        jax.ShapeDtypeStruct((count, units), bf16),
+        jax.ShapeDtypeStruct((count, 2 * units), bf16),
+    ]
+    flops = 18 * count * width * units
+    return expert_call(first_kernel, "expert_far", (even, odd, *weights), out_shape, flops)
+
+
+def expert_near(hidden, both_grad, weights):
+    count, units = hidden.shape
+    width = weights[2].shape[1]
+    out_shape = [
+        jax.ShapeDtypeStruct((count // 2, width), f32),
+        jax.ShapeDtypeStruct((count // 2, width), bf16),
+    ]
+    flops = 6 * count * width * units
+    return expert_call(second_kernel, "expert_near", (hidden, both_grad, *weights), out_shape, flops)
+
+
+def sum_kernel(chunk, even_ref, odd_ref, after_ref, kept_ref, *sent_refs):
+    del after_ref
+    rows, width = kept_ref.shape
+    for start in range(0, width, chunk):
+        cols = slice(start, start + chunk)
+        total = even_ref[:, cols] + odd_ref[:, cols].astype(f32)
+        kept_ref[:, cols] = total[:rows]
+        for i, ref in enumerate(sent_refs):
+            ref[:, cols] = total[(i + 1) * rows : (i + 2) * rows].astype(bf16)
+
+
+def sum_blocks(even, odd, after):
+    count, width = even.shape
+    rows = count // len(NEAR)
+    return pl.pallas_call(
+        functools.partial(sum_kernel, chunk_of(width, 1024)),
+        in_specs=[VMEM] * 2 + [ANY],
+        out_specs=[VMEM] * len(NEAR),
+        out_shape=[jax.ShapeDtypeStruct((rows, width), f32)]
+        + [jax.ShapeDtypeStruct((rows, width), bf16)] * (len(NEAR) - 1),
+        compiler_params=pltpu.CompilerParams(vmem_limit_bytes=16 * MIB),
+        cost_estimate=pl.CostEstimate(flops=count * width, bytes_accessed=8 * count * width, transcendentals=0),
+        name="sum_blocks",
+    )(even, odd, after)
+
+
+def exchange(send, weights):
+    by_4 = stack_rows([swap(send, 4)], send)
+    far = stack_rows([swap(send, FAR)], by_4)
+    blocks = [far] + [swap(far, k) for k in NEAR[1:]] + [send, swap(send, 2), by_4, swap(by_4, 2)]
+    even = stack_rows(blocks)
+    far_even, far_odd, *near = expert_far(even, swap(even, 1), weights)
+    near_even, near_odd = expert_near(*near, weights)
+
+    kept_far, *sent_far = sum_blocks(far_even, swap(far_odd, 1), far_odd)
+    total_far = kept_far
+    for k in (6, 2, 4):
+        total_far = total_far + swap(sent_far[NEAR.index(k) - 1], k).astype(f32)
+    kept, for_2, for_4, for_6 = sum_blocks(near_even, swap(near_odd, 1), kept_far)
+    for_4 = (for_4.astype(f32) + swap(for_6, 2).astype(f32)).astype(bf16)
+    for_2 = stack_rows([for_2], for_4)
+    return [kept, swap(for_2, 2), swap(for_4, 4), swap(total_far.astype(bf16), FAR)]
 
 
 def thirds(x):
@@ -287,9 +372,7 @@
     send = pick(routes.T, gate_probs.T, tokens, out_grad, experts)
     if experts > 1:
         send = lax.all_to_all(send, AXIS, 0, 0, axis_index_groups=peers, tiled=True)
-    even, odd = gather_rows(send.reshape(rows, width))
-    even, odd = expert_rows(even, odd, w_gate, w_up, w_down)
-    terms = scatter_sum(even, odd)
+    terms = exchange(send.reshape(rows, width), (w_gate, w_up, w_down))
     if experts > 1:
         terms = [functools.reduce(jnp.add, [t.astype(f32) for t in terms])]
     terms = [t.reshape(experts, PAIR, width) for t in terms]

time: 59.4 us -> 52.9 us (0.89)
  waiting for transfers between devices: 28.1 us -> 19.3 us
  Pallas kernels: 9.98 us -> 11.5 us
  starting transfers between devices: 19.8 us -> 21.1 us
    ppermute x16 -> x17, waiting for transfers between devices: 28.1 us -> 19.3 us  [swap(): return lax.ppermute(x, AXIS, [(i, i ^ offset) for i in range(devices)])]
    pallas_call x1 -> x8, Pallas kernels: 2.91 us -> 4.38 us  [the longest x2 4.14 us: expert_call(): pl.pallas_call(functools.partial(kernel, chunk_of(out_shape[0].shape[1],...]
    ppermute x16 -> x17, starting transfers between devices: 19.8 us -> 21.1 us  [swap(): return lax.ppermute(x, AXIS, [(i, i ^ offset) for i in range(devices)])]
  transfers between devices with their start and end apart: 16 -> 17, of which waited for: 9 -> 10; matrix products, arithmetic and copies ran while one was open for 0% -> 0% of each run, Pallas kernels for 0% -> 3%
where the time goes in v4:
time: 52.9 us; the launch traced here: 52.8 us
  starting transfers between devices  21.1 us (40%)
  waiting for transfers between devices  19.3 us (36%)
  Pallas kernels  11.5 us (22%)
  between operations  0.78 us (1%)
    ppermute x17, starting transfers between devices, swap(): return lax.ppermute(x, AXIS, [(i, i ^ offset) for i in range(devices)])  21.1 us
    ppermute x17, waiting for transfers between devices, swap(): return lax.ppermute(x, AXIS, [(i, i ^ offset) for i in range(devices)])  19.3 us
    pallas_call x2, Pallas kernels, expert_call(): pl.pallas_call(functools.partial(kernel, chunk_of(out_shape[0].shape[1],...  4.14 us
    pallas_call x1, Pallas kernels, finish(): pl.pallas_call(functools.partial(finish_kernel, experts, len(terms)), gri...  4.12 us
    pallas_call x1, Pallas kernels, pick(): pl.pallas_call(functools.partial(pick_kernel, experts, chunk), in_specs=[...  2.95 us
  transfers between devices with their start and end apart: 17, of which 10 were waited for; matrix products, arithmetic and copies ran while one was open for 0% of the time, Pallas kernels for 3%

profile of v4, /device:TPU:0, one launch (start us, length us, event | category | flops | bytes accessed | tf_op | source)
XLA Modules:
  0.0 52.8 jit_solution(5677587796565346968)
XLA Ops:
  0.7 2.9 %pick_rows.1 = bf16[1,8,7168]{2,1,0:T(8,128)(2,1)S(1)} custom-call(s32[8,128]{1,0:T(8,128)} %bitcast.17, f32[8,128]{1,0:T(8,128)} %bitcast.19, bf16[128,7168]{1,0:T(8,128)(2,1)} %tokens_ref.1, bf16[128,7168]{1,0:T(8,128)(2,1)} %grads_ref.1), custom_call_target="tpu_custom_call" | custom-call | flops 29360128 | bytes 3670016 | tf_op jit(solution)/shard_map/pick_rows/pallas_call | solution.py:125
  3.6 3.1 %collective-permute-start.1 = (bf16[8,7168]{1,0:T(8,128)(2,1)S(1)}, bf16[8,7168]{1,0:T(8,128)(2,1)S(1)}, u32[]{:S(2)}, u32[]{:S(2)}) collective-permute-start(bf16[8,7168]{1,0:T(8,128)(2,1)S(1)} %bitcast.8), channel_id=1, source_target_pairs={{0,4},{1,5},{2,6},{3,7},{4,0},{5,1},{6,2},{7,3},{8,12},{9,13},{10,... | collective-permute-start | bytes 344072 | tf_op jit(solution)/shard_map/ppermute | solution.py:32
  6.7 2.6 %collective-permute-start = (bf16[8,7168]{1,0:T(8,128)(2,1)S(1)}, bf16[8,7168]{1,0:T(8,128)(2,1)S(1)}, u32[]{:S(2)}, u32[]{:S(2)}) collective-permute-start(bf16[8,7168]{1,0:T(8,128)(2,1)S(1)} %bitcast.9), channel_id=1, source_target_pairs={{0,8},{1,9},{2,10},{3,11},{4,12},{5,13},{6,14},{7,15},{8,0},{9,1},... | collective-permute-start | bytes 344072 | tf_op jit(solution)/shard_map/ppermute | solution.py:32
  9.3 1.5 %collective-permute-start.5 = (bf16[8,7168]{1,0:T(8,128)(2,1)S(1)}, bf16[8,7168]{1,0:T(8,128)(2,1)S(1)}, u32[]{:S(2)}, u32[]{:S(2)}) collective-permute-start(bf16[8,7168]{1,0:T(8,128)(2,1)S(1)} %bitcast.10), channel_id=1, source_target_pairs={{0,2},{1,3},{2,0},{3,1},{4,6},{5,7},{6,4},{7,5},{8,10},{9,11},{10,... | collective-permute-start | bytes 344072 | tf_op jit(solution)/shard_map/ppermute | solution.py:32
  10.8 2.1 %collective-permute-start.6 = (bf16[8,7168]{1,0:T(8,128)(2,1)S(1)}, bf16[8,7168]{1,0:T(8,128)(2,1)S(1)}, u32[]{:S(2)}, u32[]{:S(2)}) collective-permute-start(bf16[8,7168]{1,0:T(8,128)(2,1)S(1)} %stack_rows.4.refs_1_.refs_6_), channel_id=1, source_target_pairs={{0,2},{1,3},{2,0},{3,1},{4,6},{5,7},{6,4},{7,5},{8,10},{9,11},{10,... | collective-permute-start | bytes 344072 | tf_op jit(solution)/shard_map/ppermute | solution.py:32
  12.9 1.8 %collective-permute-done.refs_0_ = bf16[8,7168]{1,0:T(8,128)(2,1)S(1)} collective-permute-done((bf16[8,7168]{1,0:T(8,128)(2,1)S(1)}, bf16[8,7168]{1,0:T(8,128)(2,1)S(1)}, u32[]{:S(2)}, u32[]{:S(2)}) %collective-permute-start) | collective-permute-done | bytes 114720 | tf_op jit(solution)/shard_map/ppermute | solution.py:32
  14.7 1.5 %collective-permute-start.4 = (bf16[8,7168]{1,0:T(8,128)(2,1)S(1)}, bf16[8,7168]{1,0:T(8,128)(2,1)S(1)}, u32[]{:S(2)}, u32[]{:S(2)}) collective-permute-start(bf16[8,7168]{1,0:T(8,128)(2,1)S(1)} %stack_rows.5.refs_0_), channel_id=1, source_target_pairs={{0,6},{1,7},{2,4},{3,5},{4,2},{5,3},{6,0},{7,1},{8,14},{9,15},{10,... | collective-permute-start | bytes 344072 | tf_op jit(solution)/shard_map/ppermute | solution.py:32
  16.2 1.6 %collective-permute-start.3 = (bf16[8,7168]{1,0:T(8,128)(2,1)S(1)}, bf16[8,7168]{1,0:T(8,128)(2,1)S(1)}, u32[]{:S(2)}, u32[]{:S(2)}) collective-permute-start(bf16[8,7168]{1,0:T(8,128)(2,1)S(1)} %stack_rows.5.refs_0_), channel_id=1, source_target_pairs={{0,4},{1,5},{2,6},{3,7},{4,0},{5,1},{6,2},{7,3},{8,12},{9,13},{10,... | collective-permute-start | bytes 344072 | tf_op jit(solution)/shard_map/ppermute | solution.py:32
  17.8 0.5 collective-permute-start.2
  18.3 2.2 %collective-permute-done.4.refs_3_ = bf16[8,7168]{1,0:T(8,128)(2,1)S(1)} collective-permute-done((bf16[8,7168]{1,0:T(8,128)(2,1)S(1)}, bf16[8,7168]{1,0:T(8,128)(2,1)S(1)}, u32[]{:S(2)}, u32[]{:S(2)}) %collective-permute-start.4) | collective-permute-done | bytes 114720 | tf_op jit(solution)/shard_map/ppermute | solution.py:32
  20.5 1.3 %collective-permute-done.3.refs_2_ = bf16[8,7168]{1,0:T(8,128)(2,1)S(1)} collective-permute-done((bf16[8,7168]{1,0:T(8,128)(2,1)S(1)}, bf16[8,7168]{1,0:T(8,128)(2,1)S(1)}, u32[]{:S(2)}, u32[]{:S(2)}) %collective-permute-start.3) | collective-permute-done | bytes 114720 | tf_op jit(solution)/shard_map/ppermute | solution.py:32
  21.8 0.8 %collective-permute-done.2.refs_1_ = bf16[8,7168]{1,0:T(8,128)(2,1)S(1)} collective-permute-done((bf16[8,7168]{1,0:T(8,128)(2,1)S(1)}, bf16[8,7168]{1,0:T(8,128)(2,1)S(1)}, u32[]{:S(2)}, u32[]{:S(2)}) %collective-permute-start.2) | collective-permute-done | bytes 114720 | tf_op jit(solution)/shard_map/ppermute | solution.py:32
  22.7 2.5 %collective-permute-done.7.refs_1_ = bf16[64,7168]{1,0:T(8,128)(2,1)S(1)} collective-permute-done((bf16[64,7168]{1,0:T(8,128)(2,1)S(1)}, bf16[64,7168]{1,0:T(8,128)(2,1)S(1)}, u32[]{:S(2)}, u32[]{:S(2)}) %collective-permute-start.7) | collective-permute-done | bytes 917536 | tf_op jit(solution)/shard_map/ppermute | solution.py:32
  25.2 2.6 %expert_far.1 = (f32[32,7168]{1,0:T(8,128)S(1)}, bf16[32,7168]{1,0:T(8,128)(2,1)S(1)}, bf16[64,128]{1,0:T(8,128)(2,1)S(1)}, bf16[64,256]{1,0:T(8,128)(2,1)S(1)}) custom-call(bf16[64,7168]{1,0:T(8,128)(2,1)S(1)} %stack_rows.6.refs_0_, bf16[64,7168]{1,0:T(8,128)(2,1)S(1)} %collective-permute-done.7.refs_1_, bf16[7168,128]{1,0:T(8,128)(2,1)S(1)} %copy-done, ...), custom_call_target="tpu_custom_call" | custom-call | flops 1056964608 | bytes 7340032 | tf_op jit(solution)/shard_map/expert_far/pallas_call | solution.py:199
  27.8 0.2 collective-permute-start.9
  28.0 1.5 %expert_near.1 = (f32[32,7168]{1,0:T(8,128)S(1)}, bf16[32,7168]{1,0:T(8,128)(2,1)S(1)}) custom-call(bf16[64,128]{1,0:T(8,128)(2,1)S(1)} %get-tuple-element.20.hidden_ref, bf16[64,256]{1,0:T(8,128)(2,1)S(1)} %get-tuple-element.21.both_ref, bf16[7168,128]{1,0:T(8,128)(2,1)S(1)} %copy-done, bf16[7168,128]{1,0:T(8,128)(2,1)S(1)} %copy-done.1, ...), custom_call_target="tpu_custom_call" | custom-call | flops 352321536 | bytes 5554176 | tf_op jit(solution)/shard_map/expert_near/pallas_call | solution.py:199
  29.5 0.4 collective-permute-start.8
  30.0 0.1 sum_blocks.2
  30.1 1.0 %collective-permute-start.13 = (bf16[8,7168]{1,0:T(8,128)(2,1)S(1)}, bf16[8,7168]{1,0:T(8,128)(2,1)S(1)}, u32[]{:S(2)}, u32[]{:S(2)}) collective-permute-start(bf16[8,7168]{1,0:T(8,128)(2,1)S(1)} %get-tuple-element.31), channel_id=1, source_target_pairs={{0,6},{1,7},{2,4},{3,5},{4,2},{5,3},{6,0},{7,1},{8,14},{9,15},{10,... | collective-permute-start | bytes 344072 | tf_op jit(solution)/shard_map/ppermute | solution.py:32
  31.1 1.0 %collective-permute-start.14 = (bf16[8,7168]{1,0:T(8,128)(2,1)S(1)}, bf16[8,7168]{1,0:T(8,128)(2,1)S(1)}, u32[]{:S(2)}, u32[]{:S(2)}) collective-permute-start(bf16[8,7168]{1,0:T(8,128)(2,1)S(1)} %get-tuple-element.32), channel_id=1, source_target_pairs={{0,2},{1,3},{2,0},{3,1},{4,6},{5,7},{6,4},{7,5},{8,10},{9,11},{10,... | collective-permute-start | bytes 344072 | tf_op jit(solution)/shard_map/ppermute | solution.py:32
  32.1 1.6 %collective-permute-start.15 = (bf16[8,7168]{1,0:T(8,128)(2,1)S(1)}, bf16[8,7168]{1,0:T(8,128)(2,1)S(1)}, u32[]{:S(2)}, u32[]{:S(2)}) collective-permute-start(bf16[8,7168]{1,0:T(8,128)(2,1)S(1)} %get-tuple-element.33), channel_id=1, source_target_pairs={{0,4},{1,5},{2,6},{3,7},{4,0},{5,1},{6,2},{7,3},{8,12},{9,13},{10,... | collective-permute-start | bytes 344072 | tf_op jit(solution)/shard_map/ppermute | solution.py:32
  33.7 0.1 sum_blocks.3
  33.7 0.7 %collective-permute-start.10 = (bf16[8,7168]{1,0:T(8,128)(2,1)S(1)}, bf16[8,7168]{1,0:T(8,128)(2,1)S(1)}, u32[]{:S(2)}, u32[]{:S(2)}) collective-permute-start(bf16[8,7168]{1,0:T(8,128)(2,1)S(1)} %get-tuple-element.30), channel_id=1, source_target_pairs={{0,2},{1,3},{2,0},{3,1},{4,6},{5,7},{6,4},{7,5},{8,10},{9,11},{10,... | collective-permute-start | bytes 344072 | tf_op jit(solution)/shard_map/ppermute | solution.py:32
  34.5 2.6 %collective-permute-done.13 = bf16[8,7168]{1,0:T(8,128)(2,1)S(1)} collective-permute-done((bf16[8,7168]{1,0:T(8,128)(2,1)S(1)}, bf16[8,7168]{1,0:T(8,128)(2,1)S(1)}, u32[]{:S(2)}, u32[]{:S(2)}) %collective-permute-start.13) | collective-permute-done | bytes 114720 | tf_op jit(solution)/shard_map/ppermute | solution.py:32
  37.1 1.7 %collective-permute-done.14 = bf16[8,7168]{1,0:T(8,128)(2,1)S(1)} collective-permute-done((bf16[8,7168]{1,0:T(8,128)(2,1)S(1)}, bf16[8,7168]{1,0:T(8,128)(2,1)S(1)}, u32[]{:S(2)}, u32[]{:S(2)}) %collective-permute-start.14) | collective-permute-done | bytes 114720 | tf_op jit(solution)/shard_map/ppermute | solution.py:32
  38.9 1.1 %collective-permute-start.16 = (bf16[8,7168]{1,0:T(8,128)(2,1)S(1)}, bf16[8,7168]{1,0:T(8,128)(2,1)S(1)}, u32[]{:S(2)}, u32[]{:S(2)}) collective-permute-start(bf16[8,7168]{1,0:T(8,128)(2,1)S(1)} %add_convert_fusion), channel_id=1, source_target_pairs={{0,8},{1,9},{2,10},{3,11},{4,12},{5,13},{6,14},{7,15},{8,0},{9,1},... | collective-permute-start | bytes 344072 | tf_op jit(solution)/shard_map/ppermute | solution.py:32
  39.9 0.9 %collective-permute-done.10 = bf16[8,7168]{1,0:T(8,128)(2,1)S(1)} collective-permute-done((bf16[8,7168]{1,0:T(8,128)(2,1)S(1)}, bf16[8,7168]{1,0:T(8,128)(2,1)S(1)}, u32[]{:S(2)}, u32[]{:S(2)}) %collective-permute-start.10) | collective-permute-done | bytes 114720 | tf_op jit(solution)/shard_map/ppermute | solution.py:32
  40.9 1.0 %collective-permute-start.11 = (bf16[8,7168]{1,0:T(8,128)(2,1)S(1)}, bf16[8,7168]{1,0:T(8,128)(2,1)S(1)}, u32[]{:S(2)}, u32[]{:S(2)}) collective-permute-start(bf16[8,7168]{1,0:T(8,128)(2,1)S(1)} %stack_rows.7), channel_id=1, source_target_pairs={{0,2},{1,3},{2,0},{3,1},{4,6},{5,7},{6,4},{7,5},{8,10},{9,11},{10,... | collective-permute-start | bytes 344072 | tf_op jit(solution)/shard_map/ppermute | solution.py:32
  42.0 1.3 %collective-permute-start.12 = (bf16[8,7168]{1,0:T(8,128)(2,1)S(1)}, bf16[8,7168]{1,0:T(8,128)(2,1)S(1)}, u32[]{:S(2)}, u32[]{:S(2)}) collective-permute-start(bf16[8,7168]{1,0:T(8,128)(2,1)S(1)} %add_convert_fusion.1.refs_1_), channel_id=1, source_target_pairs={{0,4},{1,5},{2,6},{3,7},{4,0},{5,1},{6,2},{7,3},{8,12},{9,13},{10,... | collective-permute-start | bytes 344072 | tf_op jit(solution)/shard_map/ppermute | solution.py:32
  43.2 3.6 %collective-permute-done.16 = bf16[8,7168]{1,0:T(8,128)(2,1)S(1)} collective-permute-done((bf16[8,7168]{1,0:T(8,128)(2,1)S(1)}, bf16[8,7168]{1,0:T(8,128)(2,1)S(1)}, u32[]{:S(2)}, u32[]{:S(2)}) %collective-permute-start.16) | collective-permute-done | bytes 114720 | tf_op jit(solution)/shard_map/ppermute | solution.py:32
  46.8 1.8 %collective-permute-done.12 = bf16[8,7168]{1,0:T(8,128)(2,1)S(1)} collective-permute-done((bf16[8,7168]{1,0:T(8,128)(2,1)S(1)}, bf16[8,7168]{1,0:T(8,128)(2,1)S(1)}, u32[]{:S(2)}, u32[]{:S(2)}) %collective-permute-start.12) | collective-permute-done | bytes 114720 | tf_op jit(solution)/shard_map/ppermute | solution.py:32
  48.6 4.1 %finish.1 = (bf16[128,7168]{1,0:T(8,128)(2,1)}, bf16[128,7168]{1,0:T(8,128)(2,1)}, f32[8,128]{1,0:T(8,128)}) custom-call(s32[8,128]{1,0:T(8,128)S(1)} %bitcast.18, f32[8,128]{1,0:T(8,128)S(1)} %bitcast.20, bf16[128,7168]{1,0:T(8,128)(2,1)S(1)} %copy-done.3, bf16[128,7168]{1,0:T(8,128)(2,1)S(1)} %copy-done.4, f32[1,8,7168]{2,1,0:T(8,128)S(1)} %bitcast.13, ...), custom_call_target="tpu_custom_call" | custom-call | flops 117440512 | bytes 7340032 | tf_op jit(solution)/shard_map/finish/pallas_call | solution.py:343
  (28 shorter events, 0.3 us)
Async XLA Ops:
  0.6 24.5 %copy-start.1 = (bf16[7168,128]{1,0:T(8,128)(2,1)S(1)}, bf16[7168,128]{1,0:T(8,128)(2,1)}, u32[]{:S(2)}) copy-start(bf16[7168,128]{1,0:T(8,128)(2,1)} %up_ref.1) | copy-start | bytes 5505028
  0.6 24.5 %copy-start.2 = (bf16[128,7168]{1,0:T(8,128)(2,1)S(1)}, bf16[128,7168]{1,0:T(8,128)(2,1)}, u32[]{:S(2)}) copy-start(bf16[128,7168]{1,0:T(8,128)(2,1)} %down_ref.1) | copy-start | bytes 5505028
  3.6 21.6 %copy-start = (bf16[7168,128]{1,0:T(8,128)(2,1)S(1)}, bf16[7168,128]{1,0:T(8,128)(2,1)}, u32[]{:S(2)}) copy-start(bf16[7168,128]{1,0:T(8,128)(2,1)} %gate_ref.1) | copy-start | bytes 5505028
  3.6 7.2 %collective-permute-start.1 = (bf16[8,7168]{1,0:T(8,128)(2,1)S(1)}, bf16[8,7168]{1,0:T(8,128)(2,1)S(1)}, u32[]{:S(2)}, u32[]{:S(2)}) collective-permute-start(bf16[8,7168]{1,0:T(8,128)(2,1)S(1)} %bitcast.8), channel_id=1, source_target_pairs={{0,4},{1,5},{2,6},{3,7},{4,0},{5,1},{6,2},{7,3},{8,12},{9,13},{10,... | collective-permute-start | bytes 344072 | tf_op jit(solution)/shard_map/ppermute | solution.py:32
  6.7 8.0 %collective-permute-start = (bf16[8,7168]{1,0:T(8,128)(2,1)S(1)}, bf16[8,7168]{1,0:T(8,128)(2,1)S(1)}, u32[]{:S(2)}, u32[]{:S(2)}) collective-permute-start(bf16[8,7168]{1,0:T(8,128)(2,1)S(1)} %bitcast.9), channel_id=1, source_target_pairs={{0,8},{1,9},{2,10},{3,11},{4,12},{5,13},{6,14},{7,15},{8,0},{9,1},... | collective-permute-start | bytes 344072 | tf_op jit(solution)/shard_map/ppermute | solution.py:32
  9.3 9.0 %collective-permute-start.5 = (bf16[8,7168]{1,0:T(8,128)(2,1)S(1)}, bf16[8,7168]{1,0:T(8,128)(2,1)S(1)}, u32[]{:S(2)}, u32[]{:S(2)}) collective-permute-start(bf16[8,7168]{1,0:T(8,128)(2,1)S(1)} %bitcast.10), channel_id=1, source_target_pairs={{0,2},{1,3},{2,0},{3,1},{4,6},{5,7},{6,4},{7,5},{8,10},{9,11},{10,... | collective-permute-start | bytes 344072 | tf_op jit(solution)/shard_map/ppermute | solution.py:32
  10.8 7.5 %collective-permute-start.6 = (bf16[8,7168]{1,0:T(8,128)(2,1)S(1)}, bf16[8,7168]{1,0:T(8,128)(2,1)S(1)}, u32[]{:S(2)}, u32[]{:S(2)}) collective-permute-start(bf16[8,7168]{1,0:T(8,128)(2,1)S(1)} %stack_rows.4.refs_1_.refs_6_), channel_id=1, source_target_pairs={{0,2},{1,3},{2,0},{3,1},{4,6},{5,7},{6,4},{7,5},{8,10},{9,11},{10,... | collective-permute-start | bytes 344072 | tf_op jit(solution)/shard_map/ppermute | solution.py:32
  14.7 5.8 %collective-permute-start.4 = (bf16[8,7168]{1,0:T(8,128)(2,1)S(1)}, bf16[8,7168]{1,0:T(8,128)(2,1)S(1)}, u32[]{:S(2)}, u32[]{:S(2)}) collective-permute-start(bf16[8,7168]{1,0:T(8,128)(2,1)S(1)} %stack_rows.5.refs_0_), channel_id=1, source_target_pairs={{0,6},{1,7},{2,4},{3,5},{4,2},{5,3},{6,0},{7,1},{8,14},{9,15},{10,... | collective-permute-start | bytes 344072 | tf_op jit(solution)/shard_map/ppermute | solution.py:32
  16.2 5.6 %collective-permute-start.3 = (bf16[8,7168]{1,0:T(8,128)(2,1)S(1)}, bf16[8,7168]{1,0:T(8,128)(2,1)S(1)}, u32[]{:S(2)}, u32[]{:S(2)}) collective-permute-start(bf16[8,7168]{1,0:T(8,128)(2,1)S(1)} %stack_rows.5.refs_0_), channel_id=1, source_target_pairs={{0,4},{1,5},{2,6},{3,7},{4,0},{5,1},{6,2},{7,3},{8,12},{9,13},{10,... | collective-permute-start | bytes 344072 | tf_op jit(solution)/shard_map/ppermute | solution.py:32
  17.8 4.8 %collective-permute-start.2 = (bf16[8,7168]{1,0:T(8,128)(2,1)S(1)}, bf16[8,7168]{1,0:T(8,128)(2,1)S(1)}, u32[]{:S(2)}, u32[]{:S(2)}) collective-permute-start(bf16[8,7168]{1,0:T(8,128)(2,1)S(1)} %stack_rows.5.refs_0_), channel_id=1, source_target_pairs={{0,2},{1,3},{2,0},{3,1},{4,6},{5,7},{6,4},{7,5},{8,10},{9,11},{10,... | collective-permute-start | bytes 344072 | tf_op jit(solution)/shard_map/ppermute | solution.py:32
  22.6 2.5 %collective-permute-start.7 = (bf16[64,7168]{1,0:T(8,128)(2,1)S(1)}, bf16[64,7168]{1,0:T(8,128)(2,1)S(1)}, u32[]{:S(2)}, u32[]{:S(2)}) collective-permute-start(bf16[64,7168]{1,0:T(8,128)(2,1)S(1)} %stack_rows.6.refs_0_), channel_id=1, source_target_pairs={{0,1},{1,0},{2,3},{3,2},{4,5},{5,4},{6,7},{7,6},{8,9},{9,8},{10,11... | collective-permute-start | bytes 2752520 | tf_op jit(solution)/shard_map/ppermute | solution.py:32
  27.8 2.2 %collective-permute-start.9 = (bf16[32,7168]{1,0:T(8,128)(2,1)S(1)}, bf16[32,7168]{1,0:T(8,128)(2,1)S(1)}, u32[]{:S(2)}, u32[]{:S(2)}) collective-permute-start(bf16[32,7168]{1,0:T(8,128)(2,1)S(1)} %get-tuple-element.25.after_ref), channel_id=1, source_target_pairs={{0,1},{1,0},{2,3},{3,2},{4,5},{5,4},{6,7},{7,6},{8,9},{9,8},{10,11... | collective-permute-start | bytes 1376264 | tf_op jit(solution)/shard_map/ppermute | solution.py:32
  29.5 4.1 %collective-permute-start.8 = (bf16[32,7168]{1,0:T(8,128)(2,1)S(1)}, bf16[32,7168]{1,0:T(8,128)(2,1)S(1)}, u32[]{:S(2)}, u32[]{:S(2)}) collective-permute-start(bf16[32,7168]{1,0:T(8,128)(2,1)S(1)} %get-tuple-element.23), channel_id=1, source_target_pairs={{0,1},{1,0},{2,3},{3,2},{4,5},{5,4},{6,7},{7,6},{8,9},{9,8},{10,11... | collective-permute-start | bytes 1376264 | tf_op jit(solution)/shard_map/ppermute | solution.py:32
  30.0 18.6 %copy-start.4 = (bf16[128,7168]{1,0:T(8,128)(2,1)S(1)}, bf16[128,7168]{1,0:T(8,128)(2,1)}, u32[]{:S(2)}) copy-start(bf16[128,7168]{1,0:T(8,128)(2,1)} %grads_ref.1) | copy-start | bytes 5505028
  30.1 18.6 %copy-start.3 = (bf16[128,7168]{1,0:T(8,128)(2,1)S(1)}, bf16[128,7168]{1,0:T(8,128)(2,1)}, u32[]{:S(2)}) copy-start(bf16[128,7168]{1,0:T(8,128)(2,1)} %tokens_ref.1) | copy-start | bytes 5505028
  30.1 18.6 %copy-start.5 = (s32[128,8]{0,1:T(8,128)S(1)}, s32[128,8]{0,1:T(8,128)}, u32[]{:S(2)}) copy-start(s32[128,8]{0,1:T(8,128)} %param.9) | copy-start | bytes 12292
  30.1 18.5 %copy-start.6 = (f32[128,8]{0,1:T(8,128)S(1)}, f32[128,8]{0,1:T(8,128)}, u32[]{:S(2)}) copy-start(f32[128,8]{0,1:T(8,128)} %param.10) | copy-start | bytes 12292
  30.1 7.0 %collective-permute-start.13 = (bf16[8,7168]{1,0:T(8,128)(2,1)S(1)}, bf16[8,7168]{1,0:T(8,128)(2,1)S(1)}, u32[]{:S(2)}, u32[]{:S(2)}) collective-permute-start(bf16[8,7168]{1,0:T(8,128)(2,1)S(1)} %get-tuple-element.31), channel_id=1, source_target_pairs={{0,6},{1,7},{2,4},{3,5},{4,2},{5,3},{6,0},{7,1},{8,14},{9,15},{10,... | collective-permute-start | bytes 344072 | tf_op jit(solution)/shard_map/ppermute | solution.py:32
  31.1 7.8 %collective-permute-start.14 = (bf16[8,7168]{1,0:T(8,128)(2,1)S(1)}, bf16[8,7168]{1,0:T(8,128)(2,1)S(1)}, u32[]{:S(2)}, u32[]{:S(2)}) collective-permute-start(bf16[8,7168]{1,0:T(8,128)(2,1)S(1)} %get-tuple-element.32), channel_id=1, source_target_pairs={{0,2},{1,3},{2,0},{3,1},{4,6},{5,7},{6,4},{7,5},{8,10},{9,11},{10,... | collective-permute-start | bytes 344072 | tf_op jit(solution)/shard_map/ppermute | solution.py:32
  32.1 6.8 %collective-permute-start.15 = (bf16[8,7168]{1,0:T(8,128)(2,1)S(1)}, bf16[8,7168]{1,0:T(8,128)(2,1)S(1)}, u32[]{:S(2)}, u32[]{:S(2)}) collective-permute-start(bf16[8,7168]{1,0:T(8,128)(2,1)S(1)} %get-tuple-element.33), channel_id=1, source_target_pairs={{0,4},{1,5},{2,6},{3,7},{4,0},{5,1},{6,2},{7,3},{8,12},{9,13},{10,... | collective-permute-start | bytes 344072 | tf_op jit(solution)/shard_map/ppermute | solution.py:32
  33.7 7.1 %collective-permute-start.10 = (bf16[8,7168]{1,0:T(8,128)(2,1)S(1)}, bf16[8,7168]{1,0:T(8,128)(2,1)S(1)}, u32[]{:S(2)}, u32[]{:S(2)}) collective-permute-start(bf16[8,7168]{1,0:T(8,128)(2,1)S(1)} %get-tuple-element.30), channel_id=1, source_target_pairs={{0,2},{1,3},{2,0},{3,1},{4,6},{5,7},{6,4},{7,5},{8,10},{9,11},{10,... | collective-permute-start | bytes 344072 | tf_op jit(solution)/shard_map/ppermute | solution.py:32
  38.9 7.9 %collective-permute-start.16 = (bf16[8,7168]{1,0:T(8,128)(2,1)S(1)}, bf16[8,7168]{1,0:T(8,128)(2,1)S(1)}, u32[]{:S(2)}, u32[]{:S(2)}) collective-permute-start(bf16[8,7168]{1,0:T(8,128)(2,1)S(1)} %add_convert_fusion), channel_id=1, source_target_pairs={{0,8},{1,9},{2,10},{3,11},{4,12},{5,13},{6,14},{7,15},{8,0},{9,1},... | collective-permute-start | bytes 344072 | tf_op jit(solution)/shard_map/ppermute | solution.py:32
  40.9 5.9 %collective-permute-start.11 = (bf16[8,7168]{1,0:T(8,128)(2,1)S(1)}, bf16[8,7168]{1,0:T(8,128)(2,1)S(1)}, u32[]{:S(2)}, u32[]{:S(2)}) collective-permute-start(bf16[8,7168]{1,0:T(8,128)(2,1)S(1)} %stack_rows.7), channel_id=1, source_target_pairs={{0,2},{1,3},{2,0},{3,1},{4,6},{5,7},{6,4},{7,5},{8,10},{9,11},{10,... | collective-permute-start | bytes 344072 | tf_op jit(solution)/shard_map/ppermute | solution.py:32
  42.0 6.7 %collective-permute-start.12 = (bf16[8,7168]{1,0:T(8,128)(2,1)S(1)}, bf16[8,7168]{1,0:T(8,128)(2,1)S(1)}, u32[]{:S(2)}, u32[]{:S(2)}) collective-permute-start(bf16[8,7168]{1,0:T(8,128)(2,1)S(1)} %add_convert_fusion.1.refs_1_), channel_id=1, source_target_pairs={{0,4},{1,5},{2,6},{3,7},{4,0},{5,1},{6,2},{7,3},{8,12},{9,13},{10,... | collective-permute-start | bytes 344072 | tf_op jit(solution)/shard_map/ppermute | solution.py:32
